TPU v7x, 256 devices: a whole 4x4x8 slice. The times are simulated.
256 devices in a mesh: tm: 4 (over x), seq: 64 (over z, y, core).
Axes of the slice: x: 4, y: 4, z: 8, core: 2. Of those that a mesh axis runs over, the one named last changes fastest.
Arguments:
- noise: float32 [2048, 64], P('seq'), may hold values from -6 to 6
- step_ids: int32 [5], replicated, may hold values from 18 to 28, as said below
- mod_table: float32 [28, 3, 3072], replicated, may hold values from -4 to 4
- embed_weight: bfloat16 [64, 3072], replicated, may hold values from -0.75 to 0.75
- qkv_weight: bfloat16 [3072, 4608], P(None, 'tm'), may hold values from -0.109375 to 0.109375
- q_gain: float32 [128], replicated, may hold values from 1.4 to 2.8
- k_gain: float32 [128], replicated, may hold values from 1.4 to 2.8
- out_weight: bfloat16 [1536, 3072], P('tm'), may hold values from -0.15625 to 0.15625
- final_weight: float32 [3072, 64], replicated, may hold values from -0.109375 to 0.109375
Outputs:
- latents: float32 [4, 2048, 64], P('tm', 'seq')
- drifts: float32 [4, 2048, 64], P('tm', 'seq')
Inputs may be any that keep to these rules, and one draw needn't show every extreme that they name: `step_ids`: strictly increasing; the last entry is 28; the gaps between neighbours are a reordering of 1, 2, 3, 4 repeated.
All inputs are finite; a program needn't handle non-finite values.
Results may differ from a plain program's by a relative error of at most 0.017.
Values may be sent and summed in bfloat16 or wider, within the bound.
A program may use at most 128 MiB of HBM per device.

v0:
```python
import jax
import jax.numpy as jnp
from jax import lax
from jax.sharding import PartitionSpec as P

HD = 128
TOTAL = 28
STEPS_DEV = 1
SWEEPS = 2


time_shift = 3.0
norm_eps = 1e-06


def prefix(part, axis, combine, identity):
    place = lax.axis_index(axis)
    gathered = lax.all_gather(part, axis)
    state = jnp.zeros_like(part) + jnp.asarray(identity, part.dtype)

    def one(turn, state):
        return combine(state, lax.dynamic_index_in_dim(gathered, turn, 0, False))

    return lax.fori_loop(0, place, one, state)


def sigma_of(step_values):
    time_left = 1.0 - step_values.astype(jnp.float32) / TOTAL
    return time_shift * time_left / (1.0 + (time_shift - 1.0) * time_left)


def rms_norm(values, gain_vector):
    return (
        values
        * lax.rsqrt(jnp.mean(values * values, axis=-1, keepdims=True) + norm_eps)
        * gain_vector
    )


def layer_norm(values):
    average = jnp.mean(values, axis=-1, keepdims=True)
    centred = values - average
    return centred * lax.rsqrt(jnp.mean(centred * centred, axis=-1, keepdims=True) + norm_eps)


def add_terms(earlier, later):
    return earlier + later


def drift_block(
    embedded, modulation, own_start, qkv_weight, q_gain, k_gain, out_weight, final_weight
):
    window, tokens_here, width = embedded.shape
    channels = final_weight.shape[1]
    heads_local = qkv_weight.shape[1] // (3 * HD)
    factor = HD ** (-0.5)
    shift_rows = modulation[:, 0][:, None, :]
    scale_rows = modulation[:, 1][:, None, :]
    modulated = (layer_norm(embedded) * (1.0 + scale_rows) + shift_rows).astype(jnp.bfloat16)
    projected = jnp.dot(
        modulated.reshape(window * tokens_here, width),
        qkv_weight,
        preferred_element_type=jnp.float32,
    )
    projected = projected.reshape(window, tokens_here, heads_local, 3, HD)
    queries = rms_norm(projected[:, :, :, 0], q_gain).astype(jnp.bfloat16)
    keys = rms_norm(projected[:, :, :, 1], k_gain).astype(jnp.bfloat16)
    values = projected[:, :, :, 2].astype(jnp.bfloat16)
    query_heads = queries.transpose(0, 2, 1, 3)
    kv_local = jnp.stack([keys, values], axis=2).reshape(window, tokens_here, 2 * heads_local * HD)
    kv_piece = lax.all_gather(kv_local, "seq", axis=1, tiled=True)
    key_count = kv_piece.shape[1]
    kv_pair = kv_piece.reshape(window, key_count, 2, heads_local, HD)
    scores = (
        jnp.einsum(
            "whqd,wkhd->whqk", query_heads, kv_pair[:, :, 0], preferred_element_type=jnp.float32
        )
        * factor
    )
    weights = jnp.exp(scores)
    numerator = jnp.einsum(
        "whqk,wkhd->whqd",
        weights.astype(jnp.bfloat16),
        kv_pair[:, :, 1],
        preferred_element_type=jnp.float32,
    )
    numerator, denominator = (numerator, jnp.sum(weights, axis=-1))
    attention = (numerator / denominator[..., None]).astype(jnp.bfloat16)
    attention = attention.transpose(0, 2, 1, 3).reshape(window, tokens_here, heads_local * HD)
    own_embedded = lax.dynamic_slice_in_dim(embedded, own_start, STEPS_DEV, 0)
    gate_all = modulation[:, 2]
    own_gate = lax.dynamic_slice_in_dim(gate_all, own_start, STEPS_DEV, 0)
    product = jnp.dot(
        attention.reshape(STEPS_DEV * lax.axis_size("tm") * tokens_here, heads_local * HD),
        out_weight,
        preferred_element_type=jnp.float32,
    )
    attended = lax.psum_scatter(
        product.reshape(STEPS_DEV * lax.axis_size("tm"), tokens_here, width),
        "tm",
        scatter_dimension=0,
        tiled=True,
    )
    combined = own_embedded + own_gate[:, None, :] * attended
    result = jnp.dot(
        combined.reshape(STEPS_DEV * tokens_here, width),
        final_weight,
        precision=lax.Precision.HIGHEST,
        preferred_element_type=jnp.float32,
    )
    return result.reshape(STEPS_DEV, tokens_here, channels)


def body(
    noise, step_ids, mod_table, embed_weight, qkv_weight, q_gain, k_gain, out_weight, final_weight
):
    tokens_here, channels = noise.shape
    width = embed_weight.shape[1]
    groups = lax.axis_size("tm")
    window = groups * STEPS_DEV
    own_start = lax.axis_index("tm") * STEPS_DEV
    sigmas = sigma_of(step_ids)
    deltas = sigmas[1:] - sigmas[:-1]
    own_delta = lax.dynamic_slice_in_dim(deltas, own_start, STEPS_DEV, 0)
    total_steps = mod_table.shape[0]
    picker = (step_ids[:window, None] == jnp.arange(total_steps, dtype=jnp.int32)[None, :]).astype(
        jnp.float32
    )
    modulation = jnp.dot(
        picker,
        mod_table.reshape(total_steps, 3 * width),
        precision=lax.Precision.HIGHEST,
        preferred_element_type=jnp.float32,
    )
    modulation = modulation.reshape(window, 3, width)
    first_embed = jnp.dot(
        noise.astype(jnp.bfloat16), embed_weight, preferred_element_type=jnp.float32
    )
    embedded = jnp.broadcast_to(first_embed[None], (window, tokens_here, width))
    gathered = noise.astype(jnp.bfloat16)[None]
    for sweep_index in range(SWEEPS):
        if sweep_index > 0:
            embedded = jnp.dot(
                gathered.reshape(window * tokens_here, channels),
                embed_weight,
                preferred_element_type=jnp.float32,
            )
            embedded = embedded.reshape(window, tokens_here, width)
        drifts = drift_block(
            embedded, modulation, own_start, qkv_weight, q_gain, k_gain, out_weight, final_weight
        )
        step_terms = own_delta[:, None, None] * drifts
        final_sweep = sweep_index + 1 == SWEEPS
        running = jnp.cumsum(step_terms, axis=0)
        before = prefix(running[-1], "tm", add_terms, jnp.zeros_like(running[-1]))
        inclusive = before[None] + running
        if not final_sweep:
            local_before = jnp.concatenate([jnp.zeros_like(running), running[:-1]], axis=0)
            own_inputs = (noise[None] + (before[None] + local_before)).astype(jnp.bfloat16)
            gathered = lax.all_gather(own_inputs, "tm", axis=0, tiled=True)
    return (noise[None] + inclusive, drifts)


def solution(mesh):
    in_specs = (P("seq", None), P(), P(), P(), P(None, "tm"), P(), P(), P("tm", None), P())
    out_specs = (P("tm", "seq", None), P("tm", "seq", None))
    return jax.shard_map(body, mesh=mesh, in_specs=in_specs, out_specs=out_specs, check_vma=False)
```

profile of v0, /device:TPU:6, one launch (start us, length us, event | category | flops | bytes accessed | tf_op | source)
XLA Modules:
  0.0 376.8 jit_solution(6482421922545877841)
XLA Ops:
  7.2 1.5 fusion.94
  11.2 1.9 dot_general.57
  13.1 2.4 fusion.16
  16.1 10.3 %copy.19 = bf16[3072,1152]{0,1:T(8,128)(2,1)} copy(bf16[3072,1152]{1,0:T(8,128)(2,1)} %param.17) | data formatting | bytes 14155776 | tf_op args[4]
  26.5 5.4 %fusion.45 = f32[4,32,3,3,128]{4,1,3,2,0:T(8,128)S(1)} fusion(bf16[3,3,128,3072,1]{3,2,1,0,4:T(8,128)(2,1)} %bitcast.203, f32[4,3072]{1,0:T(4,128)S(1)} %get-tuple-element.67, f32[4,3072]{1,0:T(4,128)S(1)} %get-tuple-element.68, f32[4,32]{1,0:T(4,128)S(1)} %add_rsqrt_fusion.5, f32[32]{0:T(128)S(1)} %broadcast_multiply_fusion.2, f32[32,3072]{1,0:T(8,128)S(1)} %copy-done.3), kind=kOutput, calls=%fused_computation.41 | convolution fusion | flops 907935744 | bytes 8159872 | tf_op jit(solution)/shard_map/dot_general | solution.py:60
  34.9 91.9 %all-gather.6.cloned.1.call-done = bf16[4,2048,768]{2,1,0:T(8,128)(2,1)} async-done(((bf16[4,32,768]{2,1,0:T(8,128)(2,1)}), bf16[4,2048,768]{2,1,0:T(8,128)(2,1)}) %all-gather.6.cloned.1.call-update) | async-done | bytes 12582928 | tf_op jit(solution)/shard_map/all_gather | solution.py:71
  126.8 15.6 %copy.22 = bf16[4,2048,768]{1,2,0:T(8,128)(2,1)} copy(bf16[4,2048,768]{2,1,0:T(8,128)(2,1)} %all-gather.6.cloned.1.call-done) | data formatting | bytes 25165824 | tf_op jit(solution)/shard_map/all_gather | solution.py:71
  142.4 4.2 %fusion.95 = (f32[4,3,32]{2,1,0:T(4,128)S(1)}, bf16[4,3,32,2048]{3,2,1,0:T(8,128)(2,1)S(1)}) fusion(bf16[4,2048,2,3,128]{1,4,3,2,0:T(8,128)(2,1)} %bitcast.199, f32[4,32,3,3,128]{4,1,3,2,0:T(8,128)} %copy-done.7, f32[128]{0:T(128)S(1)} %copy-done.17, f32[4,32,3]{1,2,0:T(4,128)S(1)} %add_rsqrt_fusion.3), kind=kOutput, calls=%fused_computation.119 | convolution fusion | flops 203832960 | bytes 8064512 | tf_op jit(solution)/shard_map/whqd,wkhd->whqk/dot_general | solution.py:75
  146.5 5.0 %fusion.39 = bf16[4,3,4,8,128]{4,3,2,1,0:T(8,128)(2,1)S(1)} fusion(bf16[4,2048,2,3,128]{1,4,3,2,0:T(8,128)(2,1)} %bitcast.200, bf16[4,3,32,2048]{3,2,1,0:T(8,128)(2,1)S(1)} %get-tuple-element.72, f32[4,32,3]{1,2,0:T(4,128)S(1)} %bitcast.214), kind=kOutput, calls=%fused_computation.38 | convolution fusion | flops 201424896 | bytes 7964160 | tf_op jit(solution)/shard_map/whqk,wkhd->whqd/dot_general | solution.py:81
  151.6 1.8 fusion.8
  156.2 21.0 %reduce-scatter.3.cloned.1.call-done = f32[1,32,3072]{2,1,0:T(8,128)} async-done(((f32[4,32,3072]{2,1,0:T(8,128)}), f32[1,32,3072]{2,1,0:T(8,128)}) %reduce-scatter.3.cloned.1.call-update) | async-done | bytes 393232 | tf_op jit(solution)/shard_map/reduce_scatter | solution.py:98
  177.2 2.3 convolution_multiply_fusion
  179.5 11.9 %all-gather = f32[128,64]{1,0:T(8,128)S(1)} all-gather(f32[32,64]{1,0:T(8,128)S(1)} %convolution_multiply_fusion), channel_id=2, replica_groups=mesh['tm'=4,'seq'=64] {'tm'}, dimensions={0}, use_global_device_ids=true | all-gather | bytes 40960 | tf_op jit(solution)/shard_map/all_gather | solution.py:18
  191.5 12.1 %all-gather.1 = bf16[128,64]{1,0:T(8,128)(2,1)S(1)} all-gather(bf16[32,64]{1,0:T(8,128)(2,1)S(1)} %add_convert_fusion.1), channel_id=3, replica_groups=mesh['tm'=4,'seq'=64] {'tm'}, dimensions={0}, use_global_device_ids=true | all-gather | bytes 20480 | tf_op jit(solution)/shard_map/all_gather | solution.py:160
  203.6 1.4 fusion.96
  205.4 5.6 %fusion = f32[4,32,3,3,128]{4,1,2,0,3:T(8,128)S(1)} fusion(bf16[3,3,128,3072,1]{3,2,1,0,4:T(8,128)(2,1)} %bitcast.204, f32[4,32,3072]{2,1,0:T(8,128)S(1)} %get-tuple-element.74, f32[4,32]{1,0:T(4,128)S(1)} %add_rsqrt_fusion.4, f32[4,32]{1,0:T(4,128)S(1)} %broadcast_multiply_fusion.1, f32[4,3072]{1,0:T(4,128)S(1)} %copy-done.11, f32[4,3072]{1,0:T(4,128)S(1)} %copy-done.13), kind=kOutput, calls=%fused_computation.2 | convolution fusion | flops 907935744 | bytes 9339904 | tf_op jit(solution)/shard_map/dot_general | solution.py:60
  214.1 90.1 %all-gather.8.cloned.1.call-done = bf16[4,2048,768]{2,1,0:T(8,128)(2,1)} async-done(((bf16[4,32,768]{2,1,0:T(8,128)(2,1)}), bf16[4,2048,768]{2,1,0:T(8,128)(2,1)}) %all-gather.8.cloned.1.call-update) | async-done | bytes 12582928 | tf_op jit(solution)/shard_map/all_gather | solution.py:71
  304.2 15.6 %copy.30 = bf16[4,2048,768]{1,2,0:T(8,128)(2,1)} copy(bf16[4,2048,768]{2,1,0:T(8,128)(2,1)} %all-gather.8.cloned.1.call-done) | data formatting | bytes 25165824 | tf_op jit(solution)/shard_map/all_gather | solution.py:71
  319.8 4.2 %fusion.97 = (f32[4,3,32]{2,1,0:T(4,128)S(1)}, bf16[4,3,32,2048]{3,2,1,0:T(8,128)(2,1)S(1)}) fusion(bf16[4,2048,2,3,128]{1,4,3,2,0:T(8,128)(2,1)} %bitcast.201, f32[4,32,3,3,128]{4,1,2,0,3:T(8,128)} %copy-done.6, f32[4,32,3]{1,2,0:T(4,128)S(1)} %add_rsqrt_fusion.1, f32[128]{0:T(128)S(1)} %copy-done.18), kind=kOutput, calls=%fused_computation.121 | convolution fusion | flops 203832960 | bytes 8064512 | tf_op jit(solution)/shard_map/whqd,wkhd->whqk/dot_general | solution.py:75
  324.0 5.0 %fusion.30 = bf16[4,3,4,8,128]{4,3,2,1,0:T(8,128)(2,1)S(1)} fusion(bf16[4,2048,2,3,128]{1,4,3,2,0:T(8,128)(2,1)} %bitcast.202, bf16[4,3,32,2048]{3,2,1,0:T(8,128)(2,1)S(1)} %get-tuple-element.76, f32[4,32,3]{1,2,0:T(4,128)S(1)} %bitcast.215), kind=kOutput, calls=%fused_computation.35 | convolution fusion | flops 201424896 | bytes 7964160 | tf_op jit(solution)/shard_map/whqk,wkhd->whqd/dot_general | solution.py:81
  329.0 1.8 fusion.6
  330.8 23.9 %reduce-scatter.5.cloned.1.call-done = f32[1,32,3072]{2,1,0:T(8,128)} async-done(((f32[4,32,3072]{2,1,0:T(8,128)}), f32[1,32,3072]{2,1,0:T(8,128)}) %reduce-scatter.5.cloned.1.call-update) | async-done | bytes 393232 | tf_op jit(solution)/shard_map/reduce_scatter | solution.py:98
  354.7 3.0 broadcast_multiply_fusion
  357.7 11.8 %all-gather.2 = f32[128,64]{1,0:T(8,128)S(1)} all-gather(f32[32,64]{1,0:T(8,128)S(1)} %get-tuple-element.77), channel_id=4, replica_groups=mesh['tm'=4,'seq'=64] {'tm'}, dimensions={0}, use_global_device_ids=true | all-gather | bytes 40960 | tf_op jit(solution)/shard_map/all_gather | solution.py:18
  (90 shorter events, 13.1 us)
Async XLA Ops:
  7.2 144.4 %copy-start = (bf16[384,3072]{1,0:T(8,128)(2,1)S(1)}, bf16[384,3072]{1,0:T(8,128)(2,1)}, u32[]{:S(2)}) copy-start(bf16[384,3072]{1,0:T(8,128)(2,1)} %param.20) | copy-start | bytes 7077892
  7.2 2.3 copy-start.5
  7.2 119.6 %all-gather.6.cloned.1.call-start = ((), (), s32[]{:S(2)}) async-start(), calls=%async_computation.2 | async-start | bytes 12779520 | tf_op jit(solution)/shard_map/all_gather | solution.py:71
  8.7 0.8 copy-start.2
  11.2 1.9 copy-start.16
  16.1 10.3 %copy-start.10 = (f32[4,3072]{1,0:T(4,128)}, f32[4,3072]{1,0:T(4,128)S(1)}, u32[]{:S(2)}) copy-start(f32[4,3072]{1,0:T(4,128)S(1)} %get-tuple-element.67) | copy-start | bytes 147460
  16.1 10.3 %copy-start.12 = (f32[4,3072]{1,0:T(4,128)}, f32[4,3072]{1,0:T(4,128)S(1)}, u32[]{:S(2)}) copy-start(f32[4,3072]{1,0:T(4,128)S(1)} %get-tuple-element.68) | copy-start | bytes 147460
  16.1 10.3 %copy-start.3 = (f32[32,3072]{1,0:T(8,128)S(1)}, f32[32,3072]{1,0:T(8,128)}, u32[]{:S(2)}) copy-start(f32[32,3072]{1,0:T(8,128)} %copy-done.2) | copy-start | bytes 1179652
  26.4 5.6 %copy-start.14 = (f32[128]{0:T(128)S(1)}, f32[128]{0:T(128)}, u32[]{:S(2)}) copy-start(f32[128]{0:T(128)} %param.19) | copy-start | bytes 1540
  31.9 0.8 copy-start.7
  33.7 143.5 %reduce-scatter.3.cloned.1.call-start = ((), (), s32[]{:S(2)}) async-start(), calls=%async_computation.3 | async-start | bytes 1966080 | tf_op jit(solution)/shard_map/reduce_scatter | solution.py:98
  34.9 107.5 %copy-start.17 = (f32[128]{0:T(128)S(1)}, f32[128]{0:T(128)}, u32[]{:S(2)}) copy-start(f32[128]{0:T(128)} %param.18) | copy-start | bytes 1540
  153.3 23.9 %copy-start.4 = (f32[3072,64]{0,1:T(8,128)S(1)}, f32[3072,64]{0,1:T(8,128)}, u32[]{:S(2)}) copy-start(f32[3072,64]{0,1:T(8,128)} %param.21) | copy-start | bytes 2359300
  153.3 38.2 %copy-start.8 = (f32[32,64]{1,0:T(8,128)S(1)}, f32[32,64]{1,0:T(8,128)}, u32[]{:S(2)}) copy-start(f32[32,64]{1,0:T(8,128)} %param.13) | copy-start | bytes 24580
  153.4 150.9 %all-gather.8.cloned.1.call-start = ((), (), s32[]{:S(2)}) async-start(), calls=%async_computation.4 | async-start | bytes 12779520 | tf_op jit(solution)/shard_map/all_gather | solution.py:71
  203.6 1.8 copy-start.11
  203.6 1.8 copy-start.13
  205.1 6.0 %copy-start.1 = (f32[4,32,3072]{2,1,0:T(8,128)}, f32[4,32,3072]{2,1,0:T(8,128)S(1)}, u32[]{:S(2)}) copy-start(f32[4,32,3072]{2,1,0:T(8,128)S(1)} %get-tuple-element.74) | copy-start | bytes 4718596
  205.4 5.9 %copy-start.15 = (f32[128]{0:T(128)S(1)}, f32[128]{0:T(128)}, u32[]{:S(2)}) copy-start(f32[128]{0:T(128)} %param.19) | copy-start | bytes 1540
  211.1 0.9 copy-start.6
  213.0 141.7 %reduce-scatter.5.cloned.1.call-start = ((), (), s32[]{:S(2)}) async-start(), calls=%async_computation.5 | async-start | bytes 1966080 | tf_op jit(solution)/shard_map/reduce_scatter | solution.py:98
  214.1 105.7 %copy-start.18 = (f32[128]{0:T(128)S(1)}, f32[128]{0:T(128)}, u32[]{:S(2)}) copy-start(f32[128]{0:T(128)} %param.18) | copy-start | bytes 1540
  330.7 23.9 %copy-start.9 = (f32[1,1,3072]{2,0,1:T(1,128)S(1)}, f32[1,1,3072]{2,0,1:T(1,128)}, u32[]{:S(2)}) copy-start(f32[1,1,3072]{2,0,1:T(1,128)} %constant_dynamic-slice_fusion) | copy-start | bytes 36868
Sparse Core Ops, SparseCore 0:
  33.8 92.8 all-gather.5
  153.5 23.7 reduce-scatter.2
  213.1 91.0 all-gather.7
  330.9 23.7 reduce-scatter.4
where the time goes:
time: 380 us; the launch traced here: 377 us
  waiting for transfers between devices  227 us (60%)
  local copies, waits for them, and re-layouts  50.8 us (13%)
  matrix products  43.5 us (11%)
  blocking collectives  35.8 us (9%)
  between operations  14.1 us (4%)
  other arithmetic  5.31 us (1%)
    all_gather x2, waiting for transfers between devices, drift_block(): kv_piece = lax.all_gather(kv_local, 'seq', axis=1, tiled=True)  182 us
    reduce_scatter x2, waiting for transfers between devices, drift_block(): lax.psum_scatter(product.reshape(STEPS_DEV * lax.axis_size('tm'), tokens_...  44.9 us
    all_gather x2, local copies, waits for them, and re-layouts, drift_block(): kv_piece = lax.all_gather(kv_local, 'seq', axis=1, tiled=True)  31.2 us
    all_gather x2, blocking collectives, prefix(): gathered = lax.all_gather(part, axis)  23.7 us
    unnamed x42, local copies, waits for them, and re-layouts  13.7 us
    all_gather x1, blocking collectives, body(): gathered = lax.all_gather(own_inputs, 'tm', axis=0, tiled=True)  12.1 us
    dot_general x2, matrix products, drift_block(): jnp.dot(modulated.reshape(window * tokens_here, width), qkv_weight, prefe...  11 us
    dot_general x2, matrix products, drift_block(): jnp.einsum('whqk,wkhd->whqd', weights.astype(jnp.bfloat16), kv_pair[:, :,...  10 us
  transfers between devices with their start and end apart: 4, of which 4 were waited for; matrix products, arithmetic and copies ran while one was open for 1% of the time, Pallas kernels for 0%

commit v1 on v0

v1 whole, which is shorter than its diff:
```python
import math

import jax
import jax.numpy as jnp
from jax import lax
from jax.experimental import pallas as pl
from jax.experimental.pallas import tpu as pltpu
from jax.sharding import PartitionSpec as P

MESH = pl.DeviceIdType.MESH
F32 = jnp.float32
BF16 = jnp.bfloat16
C = 64
D = 3072
HD = 128
HEADS = 3
WINDOW = 4
TOTAL = 28
EPS = 1e-6
PARTS = 6
DEPTH = D // PARTS
COLS = 3 * HD * HEADS
CONTRACT_LAST = (((1,), (1,)), ((), ()))


def dot(left, right):
    return jnp.dot(left, right, preferred_element_type=F32)


def dot_t(left, right):
    return lax.dot_general(left, right, CONTRACT_LAST, preferred_element_type=F32)


def split(value, pieces):
    out = []
    for _ in range(pieces):
        piece = value.astype(BF16)
        out.append(piece)
        value = value - piece.astype(F32)
    return out


def left_half(value):
    return jnp.concatenate([value, jnp.zeros_like(value)], axis=1)


def right_half(value):
    return jnp.concatenate([jnp.zeros_like(value), value], axis=1)


def kernel(
    noise_ref, ids_ref, mod_ref, e_ref, w_ref, qg_ref, kg_ref, o_ref, f_ref,
    lat_ref, dr_ref,
    noise_in, mod_in, e_in, w_in, o_in, f_in, local_sem, w_sem,
    nz, xb1, xb2, part1, part2, red, outs, acc, proj, wa, wb, bias, g12, g3, nw, efw, a_hi,
    lat_acc, dr_acc,
    a1_s, a1_r, a2_s, a2_r, r_s, r_r, b1_s, b1_r, b2_s, b2_r, o_s, o_r,
):
    c = lax.axis_index("tm")
    s = lax.axis_index("seq")
    z = s // 8
    y = (s // 2) % 4
    core = s % 2
    k = z // 2
    zlo = z % 2
    g = s % 8

    def seq_of(zz, gg):
        return zz * 8 + gg

    def device(cc, zz, gg):
        return (cc, seq_of(zz, gg))

    copies = [
        pltpu.make_async_copy(noise_ref, noise_in, local_sem.at[0]),
        pltpu.make_async_copy(e_ref, e_in, local_sem.at[1]),
        pltpu.make_async_copy(mod_ref, mod_in, local_sem.at[2]),
        pltpu.make_async_copy(f_ref, f_in, local_sem.at[3]),
        pltpu.make_async_copy(o_ref, o_in, local_sem.at[4]),
    ]
    w_copies = [
        pltpu.make_async_copy(
            w_ref.at[pl.ds(n * DEPTH, DEPTH)], w_in.at[pl.ds(n * DEPTH, DEPTH)], w_sem.at[n]
        )
        for n in range(PARTS)
    ]
    for copy in copies[:3]:
        copy.start()
    for copy in w_copies:
        copy.start()
    for copy in copies[3:]:
        copy.start()

    barrier = pltpu.get_barrier_semaphore()

    def greet(target):
        pl.semaphore_signal(barrier, inc=1, device_id=target, device_id_type=MESH)

    def greet_block(j, carry):
        greet(device((c + j % 4) % 4, 2 * ((k + j // 4) % 4) + zlo, g))
        return carry

    def greet_row(j, carry):
        greet(device((c + j) % 4, 2 * k + 1 - zlo, g))
        return carry

    def greet_column(j, carry):
        greet(device(c, 2 * ((k + j) % 4) + 1 - zlo, g))
        return carry

    def greet_plane(j, carry):
        greet(device(c, z, (g + j) % 8))
        return carry

    lax.fori_loop(1, 16, greet_block, 0)
    lax.fori_loop(0, 4, greet_row, 0)
    lax.fori_loop(1, 4, greet_column, 0)
    lax.fori_loop(1, 8, greet_plane, 0)

    copies[0].wait()
    nz[z] = jnp.concatenate([noise_in[0:16, :], noise_in[16:32, :]], axis=1)
    pl.semaphore_wait(barrier, 29)

    def a1(slot, j):
        return pltpu.make_async_remote_copy(
            src_ref=nz.at[slot], dst_ref=nz.at[slot], send_sem=a1_s.at[j], recv_sem=a1_r.at[slot],
            device_id=device(c, (z + j) % 8, g), device_id_type=MESH,
        )

    def a1_start(j, carry):
        a1(z, j).start()
        return carry

    lax.fori_loop(1, 8, a1_start, 0)

    def plane(buffer, slot, j, send, recv):
        return pltpu.make_async_remote_copy(
            src_ref=buffer.at[slot], dst_ref=buffer.at[slot], send_sem=send.at[j], recv_sem=recv.at[slot],
            device_id=device(c, z, (g + j) % 8), device_id_type=MESH,
        )

    copies[1].wait()
    embed = e_in[...].astype(F32)
    centred = embed - jnp.mean(embed, axis=1, keepdims=True)
    copies[2].wait()
    modulation = mod_in[ids_ref[k]]
    shift = modulation[0:1]
    scale = modulation[1:2]
    gate = modulation[2:3]
    scaled = split(centred * (1.0 + scale), 2)
    a_hi[0:64] = scaled[0]
    a_hi[64:128] = scaled[1]
    shifts = split(shift, 2)
    row = lax.broadcasted_iota(jnp.int32, (16, D), 0)
    zeros = jnp.zeros((16, D), BF16)
    a_hi[128:144] = jnp.where(
        row == 0, jnp.broadcast_to(shift, (16, D)),
        jnp.where(row == 1, jnp.broadcast_to(shift - shifts[0].astype(F32), (16, D)), 0.0),
    ).astype(BF16)

    def a1_wait(j, carry):
        a1((z + j) % 8, j).wait_recv()
        return carry

    lax.fori_loop(1, 8, a1_wait, 0)
    xb1[g] = nz[...].astype(BF16)

    def a2_start(j, carry):
        plane(xb1, g, j, a2_s, a2_r).start()
        return carry

    lax.fori_loop(1, 8, a2_start, 0)

    pieces = split(centred, 3)
    stacked = jnp.concatenate(pieces, axis=0)
    gram = sum(dot_t(stacked, piece) for piece in pieces)
    gram = (gram[0:64] + gram[64:128] + gram[128:192]) * (1.0 / D)
    g1, g2, gl = split(gram, 3)
    g12[0:64] = left_half(g1)
    g12[64:128] = right_half(g1)
    g12[128:192] = left_half(g2)
    g12[192:256] = right_half(g2)
    g3[0:64] = left_half(gl)
    g3[64:128] = right_half(gl)

    for n in range(PARTS):
        w_copies[n].wait()
        rows = slice(n * DEPTH, (n + 1) * DEPTH)
        for h in range(HEADS):
            cols = slice(h * 3 * HD, (h + 1) * 3 * HD)
            term = dot(a_hi[:, rows], w_in[rows, cols])
            if n == 0:
                proj[:, cols] = term
            else:
                proj[:, cols] += term
    small = proj[0:64] + proj[64:128]
    bias[...] = proj[128:136]
    small_hi, small_lo = split(small, 2)
    none = jnp.zeros((64, COLS), BF16)
    for n, value in enumerate((small_hi, none, small_lo, none)):
        wa[n * 64:(n + 1) * 64] = value
    for n, value in enumerate((none, small_hi, none, small_lo)):
        wb[n * 64:(n + 1) * 64] = value

    copies[3].wait()
    copies[4].wait()
    head_out = jnp.zeros((HEADS * HD, 2 * C), F32)
    embed_out = jnp.zeros((C, 2 * C), F32)
    for n in range(PARTS):
        rows = slice(n * DEPTH, (n + 1) * DEPTH)
        final = jnp.concatenate(split(f_in[rows], 2), axis=1)
        gated = (o_in[:, rows].astype(F32) * gate[:, rows]).astype(BF16)
        head_out += dot(gated, final)
        embed_out += dot(e_in[:, rows], final)
    head_out = head_out[:, 0:64] + head_out[:, 64:128]
    own = (c == 0).astype(F32)
    embed_out = (embed_out[:, 0:64] + embed_out[:, 64:128]) * own
    for n, value in enumerate(split(head_out, 2)):
        nw[n, 0:384] = left_half(value)
        nw[n, 384:768] = right_half(value)
    for n, value in enumerate(split(embed_out, 2)):
        efw[n * 128:n * 128 + 64] = left_half(value)
        efw[n * 128 + 64:n * 128 + 128] = right_half(value)

    gains = qg_ref[...] * kg_ref[...] * (HD ** -0.5 * math.log2(math.e))
    ones = jnp.full((HD, HD), 1.0 / HD, BF16)

    def doubled(x):
        return jnp.concatenate([x, x], axis=1)

    def inverse_deviation(x, xx):
        term = (dot(xx, g12[...]) + dot(x, g3[...])) * x.astype(F32)
        lane = lax.broadcasted_iota(jnp.int32, term.shape, 1)
        first = jnp.sum(jnp.where(lane < 64, term, 0.0), axis=1, keepdims=True)
        second = jnp.sum(jnp.where(lane < 64, 0.0, term), axis=1, keepdims=True)
        return lax.rsqrt(first + EPS), lax.rsqrt(second + EPS)

    def bias_of(start):
        return bias[0:1, start:start + HD] + bias[1:2, start:start + HD]

    def sweep(xb, recv, send, part):
        xq = jnp.concatenate([xb[g, 2 * i + zlo] for i in range(4)], axis=0)
        xxq = doubled(xq)
        ra, rb = inverse_deviation(xq, xxq)
        queries = []
        for h in range(HEADS):
            start = h * 3 * HD
            qa = dot(xxq, wa[:, start:start + HD]) * ra
            qb = dot(xxq, wb[:, start:start + HD]) * rb
            q = jnp.concatenate([qa, qb], axis=0) + bias_of(start)
            q = q * lax.rsqrt(jnp.mean(q * q, axis=1, keepdims=True) + EPS) * gains
            queries.append(q.astype(BF16))
        acc[...] = jnp.zeros_like(acc)

        def step(j, carry):
            gg = ((y + j // 2) % 4) * 2 + (core + j) % 2

            @pl.when(j > 0)
            def _():
                plane(xb, gg, j, send, recv).wait_recv()

            x = xb[gg].reshape(128, 128)
            xx = doubled(x)
            va, vb = inverse_deviation(x, xx)
            for h in range(HEADS):
                start = h * 3 * HD + HD
                kva = dot(xx, wa[:, start:start + 2 * HD]) * va
                kvb = dot(xx, wb[:, start:start + 2 * HD]) * vb
                kv = jnp.concatenate([kva, kvb], axis=0)
                keys = kv[:, 0:HD] + bias_of(start)
                values = (kv[:, HD:] + bias_of(start + HD)).astype(BF16)
                square = dot((keys * keys).astype(BF16), ones)
                keys = (keys * lax.rsqrt(square + EPS)).astype(BF16)
                weights = jnp.exp2(dot_t(queries[h], keys)).astype(BF16)
                values = jnp.concatenate([values, jnp.ones_like(values)], axis=1)
                acc[h] += dot(weights, values)
            return carry

        lax.fori_loop(0, 8, step, 0)
        attention = jnp.concatenate(
            [(acc[h, :, 0:HD] / acc[h, :, HD:]).astype(BF16) for h in range(HEADS)], axis=1
        )
        attention = jnp.concatenate([attention[0:64], attention[64:128]], axis=1)
        result = dot(attention, nw[0]) + dot(attention, nw[1]) + dot(xxq, efw[...])
        part[...] = result.reshape(4, 16, 128)

    def delta_of(t):
        def sigma(n):
            left = 1.0 - jnp.full((16, 128), n).astype(F32) / TOTAL
            return 3.0 * left / (1.0 + 2.0 * left)

        return sigma(ids_ref[t + 1]) - sigma(ids_ref[t])

    def r_copy(t, i):
        return pltpu.make_async_remote_copy(
            src_ref=part1.at[i], dst_ref=red.at[k * 4 + c], send_sem=r_s.at[t * 4 + i], recv_sem=r_r.at[k * 4 + c],
            device_id=device(i, 2 * t + zlo, g), device_id_type=MESH,
        )

    def o_copy(part, t, i):
        return pltpu.make_async_remote_copy(
            src_ref=part.at[i], dst_ref=outs.at[k * 4 + c], send_sem=o_s.at[t * 4 + i], recv_sem=o_r.at[k * 4 + c],
            device_id=device(t, 2 * i + zlo, g), device_id_type=MESH,
        )

    def each(first, act):
        def one(n, carry):
            act(n // 4, n % 4)
            return carry

        lax.fori_loop(first * 4, 16, one, 0)

    def send_out(part):
        def act(t, i):
            mine = jnp.logical_and(t == c, i == k)

            @pl.when(mine)
            def _():
                outs[k * 4 + c] = part[i]

            @pl.when(jnp.logical_not(mine))
            def _():
                o_copy(part, t, i).start()

        each(k, act)

    def wait_out(part):
        def act(t, i):
            @pl.when(jnp.logical_not(jnp.logical_and(t == c, i == k)))
            def _():
                o_copy(part, t, i).wait_send()

        each(k, act)

    def r_start(t, i):
        r_copy(t, i).start()

    def r_wait(t, i):
        r_copy(t, i).wait_send()

    @pl.when(k < 3)
    def _():
        sweep(xb1, a2_r, a2_s, part1)
        each(k + 1, r_start)

    @pl.when(k == 0)
    def _():
        send_out(part1)

    @pl.when(k == 3)
    def _():
        def wait(j, carry):
            plane(xb1, (g + j) % 8, j, a2_s, a2_r).wait_recv()
            return carry

        lax.fori_loop(1, 8, wait, 0)

    @pl.when(k > 0)
    def _():
        mine = 2 * c + zlo
        lat_acc[...] = nz[mine]
        for t in range(3):
            @pl.when(t < k)
            def _():
                for cc in range(4):
                    pltpu.make_async_remote_copy(
                        src_ref=red.at[t * 4 + cc], dst_ref=red.at[t * 4 + cc],
                        send_sem=r_s.at[0], recv_sem=r_r.at[t * 4 + cc],
                        device_id=device(cc, 2 * t + zlo, g), device_id_type=MESH,
                    ).wait_recv()
                total = (red[t * 4] + red[t * 4 + 1]) + (red[t * 4 + 2] + red[t * 4 + 3])
                lat_acc[...] += delta_of(t) * total
        xb2[g, mine] = lat_acc[...].astype(BF16)

        def b1(slot, j):
            other = (mine + j) % 8
            return pltpu.make_async_remote_copy(
                src_ref=xb2.at[g, slot], dst_ref=xb2.at[g, slot], send_sem=b1_s.at[j], recv_sem=b1_r.at[slot],
                device_id=device(other // 2, 2 * k + other % 2, g), device_id_type=MESH,
            )

        def b1_start(j, carry):
            b1(mine, j).start()
            return carry

        def b1_wait(j, carry):
            b1((mine + j) % 8, j).wait_recv()
            return carry

        def b1_sent(j, carry):
            b1(mine, j).wait_send()
            return carry

        def b2_start(j, carry):
            plane(xb2, g, j, b2_s, b2_r).start()
            return carry

        def b2_sent(j, carry):
            plane(xb2, g, j, b2_s, b2_r).wait_send()
            return carry

        lax.fori_loop(1, 8, b1_start, 0)
        lax.fori_loop(1, 8, b1_wait, 0)
        lax.fori_loop(1, 8, b2_start, 0)
        sweep(xb2, b2_r, b2_s, part2)
        send_out(part2)
        lax.fori_loop(1, 8, b1_sent, 0)
        lax.fori_loop(1, 8, b2_sent, 0)
        wait_out(part2)

    def a_sent(j, carry):
        a1(z, j).wait_send()
        plane(xb1, g, j, a2_s, a2_r).wait_send()
        return carry

    lax.fori_loop(1, 8, a_sent, 0)

    @pl.when(k < 3)
    def _():
        each(k + 1, r_wait)

    @pl.when(k == 0)
    def _():
        wait_out(part1)

    lat_acc[...] = nz[z]
    for t in range(4):
        @pl.when(t <= c)
        def _():
            for cc in range(4):
                @pl.when(jnp.logical_not(jnp.logical_and(t == k, cc == c)))
                def _():
                    pltpu.make_async_remote_copy(
                        src_ref=outs.at[t * 4 + cc], dst_ref=outs.at[t * 4 + cc],
                        send_sem=o_s.at[0], recv_sem=o_r.at[t * 4 + cc],
                        device_id=device(cc, 2 * t + zlo, g), device_id_type=MESH,
                    ).wait_recv()
            total = (outs[t * 4] + outs[t * 4 + 1]) + (outs[t * 4 + 2] + outs[t * 4 + 3])
            lat_acc[...] += delta_of(t) * total
            dr_acc[...] = total
    lat_ref[0, 0:16, :] = lat_acc[:, 0:64]
    lat_ref[0, 16:32, :] = lat_acc[:, 64:128]
    dr_ref[0, 0:16, :] = dr_acc[:, 0:64]
    dr_ref[0, 16:32, :] = dr_acc[:, 64:128]


def body(
    noise, step_ids, mod_table, embed_weight, qkv_weight, q_gain, k_gain, out_weight, final_weight
):
    anywhere = pl.BlockSpec(memory_space=pl.ANY)
    vmem = pl.BlockSpec(memory_space=pltpu.VMEM)
    out = jax.ShapeDtypeStruct((1, 32, C), F32)
    dma = pltpu.SemaphoreType.DMA
    return pl.pallas_call(
        kernel,
        out_shape=(out, out),
        in_specs=[
            anywhere, pl.BlockSpec(memory_space=pltpu.SMEM), anywhere, anywhere, anywhere,
            vmem, vmem, anywhere, anywhere,
        ],
        out_specs=(vmem, vmem),
        scratch_shapes=[
            pltpu.VMEM((32, C), F32),
            pltpu.VMEM((TOTAL, 3, D), F32),
            pltpu.VMEM((C, D), BF16),
            pltpu.VMEM((D, COLS), BF16),
            pltpu.VMEM((HEADS * HD, D), BF16),
            pltpu.VMEM((D, C), F32),
            dma((5,)),
            dma((PARTS,)),
            pltpu.VMEM((8, 16, 128), F32),
            pltpu.VMEM((8, 8, 16, 128), BF16),
            pltpu.VMEM((8, 8, 16, 128), BF16),
            pltpu.VMEM((4, 16, 128), F32),
            pltpu.VMEM((4, 16, 128), F32),
            pltpu.VMEM((12, 16, 128), F32),
            pltpu.VMEM((16, 16, 128), F32),
            pltpu.VMEM((HEADS, 128, 2 * HD), F32),
            pltpu.VMEM((144, COLS), F32),
            pltpu.VMEM((256, COLS), BF16),
            pltpu.VMEM((256, COLS), BF16),
            pltpu.VMEM((8, COLS), F32),
            pltpu.VMEM((256, 128), BF16),
            pltpu.VMEM((128, 128), BF16),
            pltpu.VMEM((2, 768, 128), BF16),
            pltpu.VMEM((256, 128), BF16),
            pltpu.VMEM((144, D), BF16),
            pltpu.VMEM((16, 128), F32),
            pltpu.VMEM((16, 128), F32),
            dma((8,)), dma((8,)), dma((8,)), dma((8,)), dma((16,)), dma((12,)),
            dma((8,)), dma((8,)), dma((8,)), dma((8,)), dma((16,)), dma((16,)),
        ],
        compiler_params=pltpu.CompilerParams(
            collective_id=0, has_side_effects=True, vmem_limit_bytes=50 * 1024 * 1024
        ),
        cost_estimate=pl.CostEstimate(flops=4_000_000_000, bytes_accessed=14_000_000, transcendentals=1_700_000),
    )(
        noise, step_ids, mod_table, embed_weight, qkv_weight,
        q_gain.reshape(1, HD), k_gain.reshape(1, HD), out_weight, final_weight,
    )


def solution(mesh):
    in_specs = (P("seq", None), P(), P(), P(), P(None, "tm"), P(), P(), P("tm", None), P())
    out_specs = (P("tm", "seq", None), P("tm", "seq", None))
    return jax.shard_map(body, mesh=mesh, in_specs=in_specs, out_specs=out_specs, check_vma=False)
```

time: 380 us -> 71.6 us (0.19)
  waiting for transfers between devices: 227 us -> 0 us
  Pallas kernels: 0 us -> 65.9 us
  local copies, waits for them, and re-layouts: 50.8 us -> 4.86 us
  matrix products: 43.5 us -> 0 us
  blocking collectives: 35.8 us -> 0 us
  between operations: 14.1 us -> 0.73 us
  other arithmetic: 5.31 us -> 0 us
    all_gather x2 -> x0, waiting for transfers between devices: 182 us -> none  [drift_block(): kv_piece = lax.all_gather(kv_local, 'seq', axis=1, tiled=True)]
    pallas_call x0 -> x1, Pallas kernels: none -> 65.9 us  [body(): pl.pallas_call(kernel, out_shape=(out, out), in_specs=[anywhere, pl.Block...]
    reduce_scatter x2 -> x0, waiting for transfers between devices: 44.9 us -> none  [drift_block(): lax.psum_scatter(product.reshape(STEPS_DEV * lax.axis_size('tm'), tokens_...]
    dot_general x13 -> x0, matrix products: 43.5 us -> none  [the longest x2 11 us: drift_block(): jnp.dot(modulated.reshape(window * tokens_here, width), qkv_weight, prefe...]
    all_gather x3 -> x0, blocking collectives: 35.8 us -> none  [the longest x2 23.7 us: prefix(): gathered = lax.all_gather(part, axis)]
    all_gather x2 -> x0, local copies, waits for them, and re-layouts: 31.2 us -> none  [drift_block(): kv_piece = lax.all_gather(kv_local, 'seq', axis=1, tiled=True)]
    unnamed x42 -> x14, local copies, waits for them, and re-layouts: 13.7 us -> 4.86 us
  transfers between devices with their start and end apart: 4 -> 0, of which waited for: 4 -> 0; matrix products, arithmetic and copies ran while one was open for 1% -> 0% of each run, Pallas kernels for 0% -> 0%
where the time goes in v1:
time: 71.6 us; the launch traced here: 71.5 us
  Pallas kernels  65.9 us (92%)
  local copies, waits for them, and re-layouts  4.86 us (7%)
  between operations  0.73 us (1%)
    pallas_call x1, Pallas kernels, body(): pl.pallas_call(kernel, out_shape=(out, out), in_specs=[anywhere, pl.Block...  65.9 us
    unnamed x14, local copies, waits for them, and re-layouts  4.86 us

profile of v1, /device:TPU:6, one launch (start us, length us, event | category | flops | bytes accessed | tf_op | source)
XLA Modules:
  0.0 71.5 jit_solution(15796936714279631747)
XLA Ops:
  0.6 2.0 %copy.11.mod_ref = f32[28,3,3072]{2,1,0:T(4,128)S(1)} copy(f32[28,3,3072]{2,0,1:T(8,128)} %param.11) | data formatting | bytes 2064384 | tf_op args[2]
  2.6 0.0 copy-start
  2.6 0.0 copy-start.1
  2.6 0.0 copy-start.2
  2.6 0.0 copy-start.3
  2.7 0.0 copy-start.4
  2.7 1.6 %copy.12.f_ref = f32[3072,64]{1,0:T(8,128)S(1)} copy(f32[3072,64]{0,1:T(8,128)} %param.17) | data formatting | bytes 1572864 | tf_op args[8]
  4.3 0.0 copy-done
  4.3 0.0 copy-done.1
  4.3 0.0 copy-done.2
  4.3 0.0 copy-done.3
  4.4 0.0 copy-done.4
  4.4 65.9 %shard_map.104 = (f32[1,32,64]{2,1,0:T(8,128)S(1)}, f32[1,32,64]{2,1,0:T(8,128)S(1)}) custom-call(f32[32,64]{1,0:T(8,128)S(1)} %copy-done.1, s32[5]{0:T(128)S(1)} %copy-done.2, f32[28,3,3072]{2,1,0:T(4,128)S(1)} %copy.11.mod_ref, bf16[64,3072]{1,0:T(8,128)(2,1)S(1)} %copy-done, bf16[3072,1152]{1,0:T(8,128)(2,1)} %w_ref.1, f32[1,128]{1,0:T(1,128)S(1)} %bitcast.2, ...), custom_call_target="tpu_custom_call" | custom-call | flops 4000000000 | bytes 14000000 | tf_op jit(solution)/shard_map/pallas_call | solution.py:454
  70.3 0.6 copy.15
  70.9 0.6 copy.16
Async XLA Ops:
  2.6 1.7 %copy-start = (bf16[64,3072]{1,0:T(8,128)(2,1)S(1)}, bf16[64,3072]{1,0:T(8,128)(2,1)}, u32[]{:S(2)}) copy-start(bf16[64,3072]{1,0:T(8,128)(2,1)} %e_ref.1) | copy-start | bytes 1179652
  2.6 1.7 %copy-start.1 = (f32[32,64]{1,0:T(8,128)S(1)}, f32[32,64]{1,0:T(8,128)}, u32[]{:S(2)}) copy-start(f32[32,64]{1,0:T(8,128)} %noise_ref.1) | copy-start | bytes 24580
  2.6 1.7 %copy-start.2 = (s32[5]{0:T(128)S(1)}, s32[5]{0:T(128)}, u32[]{:S(2)}) copy-start(s32[5]{0:T(128)} %ids_ref.1) | copy-start | bytes 64
  2.6 1.7 %copy-start.3 = (f32[128]{0:T(128)S(1)}, f32[128]{0:T(128)}, u32[]{:S(2)}) copy-start(f32[128]{0:T(128)} %param.14) | copy-start | bytes 1540
  2.7 1.7 %copy-start.4 = (f32[128]{0:T(128)S(1)}, f32[128]{0:T(128)}, u32[]{:S(2)}) copy-start(f32[128]{0:T(128)} %param.15) | copy-start | bytes 1540

commit v2 on v1

v2 whole, which is shorter than its diff:
```python
import math

import jax
import jax.numpy as jnp
from jax import lax
from jax.experimental import pallas as pl
from jax.experimental.pallas import tpu as pltpu
from jax.sharding import PartitionSpec as P

MESH = pl.DeviceIdType.MESH
F32 = jnp.float32
BF16 = jnp.bfloat16
C = 64
D = 3072
HD = 128
HEADS = 3
WINDOW = 4
TOTAL = 28
EPS = 1e-6
PARTS = 6
DEPTH = D // PARTS
COLS = 3 * HD * HEADS
FAR_FIRST = sorted(
    [(a, b) for a in range(8) for b in range(4) if a or b],
    key=lambda ab: -(min(ab[0], 8 - ab[0]) + min(ab[1], 4 - ab[1])),
)
CONTRACT_LAST = (((1,), (1,)), ((), ()))


def dot(left, right):
    return jnp.dot(left, right, preferred_element_type=F32)


def dot_t(left, right):
    return lax.dot_general(left, right, CONTRACT_LAST, preferred_element_type=F32)


def split(value, pieces):
    out = []
    for _ in range(pieces):
        piece = value.astype(BF16)
        out.append(piece)
        value = value - piece.astype(F32)
    return out


def left_half(value):
    return jnp.concatenate([value, jnp.zeros_like(value)], axis=1)


def right_half(value):
    return jnp.concatenate([jnp.zeros_like(value), value], axis=1)


def kernel(
    noise_ref, ids_in, mod_ref, e_ref, w_ref, qgain_ref, kgain_ref, o_ref, f_ref,
    out_ref,
    noise_in, ids_ref, mod_in, e_in, w_in, qg_ref, kg_ref, o_in, f_in, local_sem, w_sem,
    own_noise, red_noise, xb1, xb2, keys_ref, values_ref, part1, part2, red, outs,
    proj, wa, wb, bias, g12, g3, nw, efw, a_hi, lat_acc, dr_acc,
    a_s, a_r, n_s, n_r, h_s, h_r, r_s, r_r, b_s, b_r, o_s, o_r,
):
    c = lax.axis_index("tm")
    s = lax.axis_index("seq")
    z = s // 8
    y = (s // 2) % 4
    core = s % 2

    def device(cc, zz, yy):
        return (cc % 4, (zz % 8) * 8 + (yy % 4) * 2 + core)

    slot = y * 8 + z
    mine = c * 8 + z
    sibling = (c, z * 8 + y * 2 + 1 - core)

    noise_copy = pltpu.make_async_copy(noise_ref, noise_in, local_sem.at[0])
    noise_copy.start()

    barrier = pltpu.get_barrier_semaphore()

    def greet(target):
        pl.semaphore_signal(barrier, inc=1, device_id=target, device_id_type=MESH)

    for dz, dy in FAR_FIRST:
        greet(device(c, z + dz, y + dy))
    for dz, dx in FAR_FIRST:
        if dx:
            greet(device(c + dx, z + dz, y))
    for dx in range(1, 4):
        for dy in range(1, 4):
            greet(device(c + dx, z, y + dy))
    greet(sibling)

    copies = [
        pltpu.make_async_copy(e_ref, e_in, local_sem.at[1]),
        pltpu.make_async_copy(ids_in, ids_ref, local_sem.at[2]),
        pltpu.make_async_copy(mod_ref, mod_in, local_sem.at[3]),
        pltpu.make_async_copy(f_ref, f_in, local_sem.at[4]),
        pltpu.make_async_copy(o_ref, o_in, local_sem.at[5]),
        pltpu.make_async_copy(qgain_ref, qg_ref, local_sem.at[6]),
        pltpu.make_async_copy(kgain_ref, kg_ref, local_sem.at[7]),
    ]
    w_copies = [
        pltpu.make_async_copy(
            w_ref.at[pl.ds(n * DEPTH, DEPTH)], w_in.at[pl.ds(n * DEPTH, DEPTH)], w_sem.at[n]
        )
        for n in range(PARTS)
    ]

    for copy in copies[:3] + w_copies + copies[3:]:
        copy.start()

    def small_matrices():
        copies[0].wait()
        embed = e_in[...].astype(F32)
        centred = embed - jnp.mean(embed, axis=1, keepdims=True)
        copies[1].wait()
        copies[2].wait()
        here = pl.ds(ids_ref[y], 1)
        shift = mod_in[0, here]
        scale = mod_in[1, here]
        gate = mod_in[2, here]
        scaled = split(centred * (1.0 + scale), 2)
        a_hi[0:64] = scaled[0]
        a_hi[64:128] = scaled[1]
        shifts = split(shift, 2)
        row = lax.broadcasted_iota(jnp.int32, (16, D), 0)
        a_hi[128:144] = jnp.where(
            row == 0, jnp.broadcast_to(shift, (16, D)),
            jnp.where(row == 1, jnp.broadcast_to(shift - shifts[0].astype(F32), (16, D)), 0.0),
        ).astype(BF16)

        pieces = split(centred, 3)
        stacked = jnp.concatenate(pieces, axis=0)
        gram = dot_t(stacked, stacked)
        gram = gram[0:64] + gram[64:128] + gram[128:192]
        gram = (gram[:, 0:64] + gram[:, 64:128] + gram[:, 128:192]) * (1.0 / D)
        g1, g2, gl = split(gram, 3)
        g12[0:64] = left_half(g1)
        g12[64:128] = right_half(g1)
        g12[128:192] = left_half(g2)
        g12[192:256] = right_half(g2)
        g3[0:64] = left_half(gl)
        g3[64:128] = right_half(gl)

        for copy in w_copies:
            copy.wait()
        proj[...] = dot(a_hi[...], w_in[...])
        small = proj[0:64] + proj[64:128]
        bias[...] = proj[128:136]
        small_hi, small_lo = split(small, 2)
        none = jnp.zeros((64, COLS), BF16)
        for n, value in enumerate((small_hi, none, small_lo, none)):
            wa[n * 64:(n + 1) * 64] = value
        for n, value in enumerate((none, small_hi, none, small_lo)):
            wb[n * 64:(n + 1) * 64] = value

        values_ref[:, :, HD:] = jnp.ones((HEADS, 2048, HD), BF16)
        for copy in copies[3:]:
            copy.wait()
        final = f_in[...]
        final_hl = jnp.concatenate(split(final, 2), axis=0)
        gated_hl = jnp.concatenate(split(final * gate, 2), axis=0)
        head_out = dot_t(o_in[...], gated_hl)
        embed_out = dot_t(e_in[...], final_hl)
        head_out = head_out[:, 0:64] + head_out[:, 64:128]
        own = (c == 0).astype(F32)
        embed_out = (embed_out[:, 0:64] + embed_out[:, 64:128]) * own
        for n, value in enumerate(split(head_out, 2)):
            nw[n, 0:384] = left_half(value)
            nw[n, 384:768] = right_half(value)
        for n, value in enumerate(split(embed_out, 2)):
            efw[n * 128:n * 128 + 64] = left_half(value)
            efw[n * 128 + 64:n * 128 + 128] = right_half(value)

    @pl.when(z < 4)
    def _():
        small_matrices()

    noise_copy.wait()
    packed = jnp.concatenate([noise_in[0:16], noise_in[16:32]], axis=1)
    own_noise[...] = packed
    xb1[core, slot] = packed.astype(BF16)
    pl.semaphore_wait(barrier, 65)

    def block_copy(buffer, where, target, send, recv):
        return pltpu.make_async_remote_copy(
            src_ref=buffer.at[core, where], dst_ref=buffer.at[core, where], send_sem=send, recv_sem=recv,
            device_id=target, device_id_type=MESH,
        )

    def blocks(buffer, count, send, recv):
        part = buffer.at[core, pl.ds(0, count)]
        return pltpu.make_async_remote_copy(
            src_ref=part, dst_ref=part, send_sem=send, recv_sem=recv, device_id=sibling, device_id_type=MESH,
        )

    def a_send(dz, yy):
        block_copy(xb1, slot, device(c, z + dz, yy), a_s.at[0], a_r.at[0]).start()

    for dz in (4, 3, 5, 2, 6, 1, 7):
        for yy in range(3):
            a_send(dz, yy)
    for yy in range(3):
        @pl.when(y != yy)
        def _():
            a_send(0, yy)

    def n_copy(t):
        return pltpu.make_async_remote_copy(
            src_ref=own_noise, dst_ref=red_noise, send_sem=n_s.at[t], recv_sem=n_r.at[0],
            device_id=device(c, z, t), device_id_type=MESH,
        )

    @pl.when(y == c)
    def _():
        red_noise[...] = own_noise[...]
        for t in range(1, WINDOW):
            @pl.when(y != t)
            def _():
                n_copy(t).start()

    @pl.when(z >= 4)
    def _():
        small_matrices()

    ones = jnp.full((HD, HD), 1.0 / HD, BF16)

    def doubled(x):
        return jnp.concatenate([x, x], axis=1)

    def inverse_deviation(x, xx):
        term = (dot(xx, g12[...]) + dot(x, g3[...])) * x.astype(F32)
        lane = lax.broadcasted_iota(jnp.int32, term.shape, 1)
        first = jnp.sum(jnp.where(lane < 64, term, 0.0), axis=1, keepdims=True)
        second = jnp.sum(jnp.where(lane < 64, 0.0, term), axis=1, keepdims=True)
        return lax.rsqrt(first + EPS), lax.rsqrt(second + EPS)

    def bias_of(start):
        return bias[0:1, start:start + HD] + bias[1:2, start:start + HD]

    def project(x, first):
        xx = doubled(x)
        va, vb = inverse_deviation(x, xx)
        rows = slice(first * 1024, (first + 1) * 1024)
        for h in range(HEADS):
            start = h * 3 * HD + HD
            kva = dot(xx, wa[:, start:start + 2 * HD]) * va
            kvb = dot(xx, wb[:, start:start + 2 * HD]) * vb
            kv = jnp.concatenate([kva, kvb], axis=0)
            keys = kv[:, 0:HD] + bias_of(start)
            square = dot((keys * keys).astype(BF16), ones)
            keys_ref[h, rows] = (keys * lax.rsqrt(square + EPS)).astype(BF16)
            values_ref[h, rows, 0:HD] = (kv[:, HD:] + bias_of(start + HD)).astype(BF16)

    def half_copy(buffer, which, send, recv):
        return pltpu.make_async_remote_copy(
            src_ref=buffer.at[which], dst_ref=buffer.at[which], send_sem=send, recv_sem=recv,
            device_id=sibling, device_id_type=MESH,
        )

    def sweep(xb, sweep_index, send, recv, part):
        blocks(xb, 31, send, recv).wait_recv()
        half_copy(xb, core, h_s.at[sweep_index], h_r.at[sweep_index]).start()
        gains = qg_ref[...] * kg_ref[...] * (HD ** -0.5 * math.log2(math.e))
        xq = jnp.concatenate([xb[core, i * 8 + z] for i in range(4)], axis=0)
        xxq = doubled(xq)
        ra, rb = inverse_deviation(xq, xxq)
        queries = []
        for h in range(HEADS):
            start = h * 3 * HD
            qa = dot(xxq, wa[:, start:start + HD]) * ra
            qb = dot(xxq, wb[:, start:start + HD]) * rb
            q = jnp.concatenate([qa, qb], axis=0) + bias_of(start)
            q = q * lax.rsqrt(jnp.mean(q * q, axis=1, keepdims=True) + EPS) * gains
            queries.append(q.astype(BF16))
        project(xb[core].reshape(512, 128), 0)
        half_copy(xb, 1 - core, h_s.at[sweep_index], h_r.at[sweep_index]).wait_recv()
        project(xb[1 - core].reshape(512, 128), 1)
        heads = []
        for h in range(HEADS):
            weights = jnp.exp2(dot_t(queries[h], keys_ref[h])).astype(BF16)
            summed = dot(weights, values_ref[h])
            heads.append((summed[:, 0:HD] / summed[:, HD:]).astype(BF16))
        attention = jnp.concatenate(heads, axis=1)
        attention = jnp.concatenate([attention[0:64], attention[64:128]], axis=1)
        result = dot(attention, nw[0]) + dot(attention, nw[1]) + dot(xxq, efw[...])
        part[...] = result.reshape(4, 16, 128)

    def delta_of(t):
        def sigma(n):
            left = 1.0 - jnp.full((16, 128), n).astype(F32) / TOTAL
            return 3.0 * left / (1.0 + 2.0 * left)

        return sigma(ids_ref[t + 1]) - sigma(ids_ref[t])

    def r_copy(t, i):
        return pltpu.make_async_remote_copy(
            src_ref=part1.at[i], dst_ref=red.at[y * 4 + c], send_sem=r_s.at[t * 4 + i], recv_sem=r_r.at[y * 4 + c],
            device_id=device(i, z, t), device_id_type=MESH,
        )

    def o_copy(part, t, i):
        return pltpu.make_async_remote_copy(
            src_ref=part.at[i], dst_ref=outs.at[y * 4 + c], send_sem=o_s.at[t * 4 + i], recv_sem=o_r.at[y * 4 + c],
            device_id=device(t, z, i), device_id_type=MESH,
        )

    def each(first, act):
        count = 4 - first

        def one(n, carry):
            act(first + n % count, n // count)
            return carry

        lax.fori_loop(0, 4 * count, one, 0)

    def send_out(part):
        def act(t, i):
            mine = jnp.logical_and(t == c, i == y)

            @pl.when(mine)
            def _():
                outs[y * 4 + c] = part[i]

            @pl.when(jnp.logical_not(mine))
            def _():
                o_copy(part, t, i).start()

        each(y, act)

    def wait_out(part):
        def act(t, i):
            @pl.when(jnp.logical_not(jnp.logical_and(t == c, i == y)))
            def _():
                o_copy(part, t, i).wait_send()

        each(y, act)

    def r_start(t, i):
        r_copy(t, i).start()

    def r_wait(t, i):
        r_copy(t, i).wait_send()

    @pl.when(y < 3)
    def _():
        sweep(xb1, 0, a_s.at[0], a_r.at[0], part1)
        each(y + 1, r_start)

    @pl.when(y == 0)
    def _():
        send_out(part1)

    @pl.when(y > 0)
    def _():
        @pl.when(y != c)
        def _():
            n_copy(y).wait_recv()

        lat_acc[...] = red_noise[...]
        for t in range(3):
            @pl.when(t < y)
            def _():
                for cc in range(4):
                    pltpu.make_async_remote_copy(
                        src_ref=red.at[t * 4 + cc], dst_ref=red.at[t * 4 + cc],
                        send_sem=r_s.at[0], recv_sem=r_r.at[t * 4 + cc],
                        device_id=device(cc, z, t), device_id_type=MESH,
                    ).wait_recv()
                total = (red[t * 4] + red[t * 4 + 1]) + (red[t * 4 + 2] + red[t * 4 + 3])
                lat_acc[...] += delta_of(t) * total
        xb2[core, mine] = lat_acc[...].astype(BF16)
        for dz, dx in FAR_FIRST:
            block_copy(xb2, mine, device(c + dx, z + dz, y), b_s.at[0], b_r.at[0]).start()
        sweep(xb2, 1, b_s.at[0], b_r.at[0], part2)
        send_out(part2)

    lat_acc[...] = own_noise[...]
    for t in range(4):
        @pl.when(t <= c)
        def _():
            for cc in range(4):
                @pl.when(jnp.logical_not(jnp.logical_and(t == y, cc == c)))
                def _():
                    pltpu.make_async_remote_copy(
                        src_ref=outs.at[t * 4 + cc], dst_ref=outs.at[t * 4 + cc],
                        send_sem=o_s.at[0], recv_sem=o_r.at[t * 4 + cc],
                        device_id=device(cc, z, t), device_id_type=MESH,
                    ).wait_recv()
            total = (outs[t * 4] + outs[t * 4 + 1]) + (outs[t * 4 + 2] + outs[t * 4 + 3])
            lat_acc[...] += delta_of(t) * total
            dr_acc[...] = total
    out_ref[0:16, 0:C] = lat_acc[:, 0:C]
    out_ref[16:32, 0:C] = lat_acc[:, C:]
    out_ref[0:16, C:] = dr_acc[:, 0:C]
    out_ref[16:32, C:] = dr_acc[:, C:]
    @pl.when(y < 3)
    def _():
        blocks(xb1, 23, a_s.at[0], a_r.at[0]).wait_send()
        half_copy(xb1, core, h_s.at[0], h_r.at[0]).wait_send()
        each(y + 1, r_wait)

    @pl.when(y == 3)
    def _():
        blocks(xb1, 24, a_s.at[0], a_r.at[0]).wait_send()

    @pl.when(y == 0)
    def _():
        wait_out(part1)

    @pl.when(y > 0)
    def _():
        blocks(xb2, 31, b_s.at[0], b_r.at[0]).wait_send()
        half_copy(xb2, core, h_s.at[1], h_r.at[1]).wait_send()
        wait_out(part2)

    @pl.when(y == c)
    def _():
        for t in range(1, WINDOW):
            @pl.when(y != t)
            def _():
                n_copy(t).wait_send()


def body(
    noise, step_ids, mod_table, embed_weight, qkv_weight, q_gain, k_gain, out_weight, final_weight
):
    hbm = pl.BlockSpec(memory_space=pltpu.HBM)
    vmem = pl.BlockSpec(memory_space=pltpu.VMEM)
    out = pltpu.VMEM((32, 2 * C), F32)
    dma = pltpu.SemaphoreType.DMA
    both = pl.pallas_call(
        kernel,
        out_shape=out,
        in_specs=[hbm] * 9,
        out_specs=vmem,
        scratch_shapes=[
            pltpu.VMEM((32, C), F32),
            pltpu.SMEM((WINDOW + 1,), jnp.int32),
            pltpu.VMEM((3, TOTAL, D), F32),
            pltpu.VMEM((C, D), BF16),
            pltpu.VMEM((D, COLS), BF16),
            pltpu.VMEM((1, HD), F32),
            pltpu.VMEM((1, HD), F32),
            pltpu.VMEM((HEADS * HD, D), BF16),
            pltpu.VMEM((C, D), F32),
            dma((8,)),
            dma((PARTS,)),
            pltpu.VMEM((16, 128), F32),
            pltpu.VMEM((16, 128), F32),
            pltpu.VMEM((2, 32, 16, 128), BF16),
            pltpu.VMEM((2, 32, 16, 128), BF16),
            pltpu.VMEM((HEADS, 2048, HD), BF16),
            pltpu.VMEM((HEADS, 2048, 2 * HD), BF16),
            pltpu.VMEM((4, 16, 128), F32),
            pltpu.VMEM((4, 16, 128), F32),
            pltpu.VMEM((12, 16, 128), F32),
            pltpu.VMEM((16, 16, 128), F32),
            pltpu.VMEM((144, COLS), F32),
            pltpu.VMEM((256, COLS), BF16),
            pltpu.VMEM((256, COLS), BF16),
            pltpu.VMEM((8, COLS), F32),
            pltpu.VMEM((256, 128), BF16),
            pltpu.VMEM((128, 128), BF16),
            pltpu.VMEM((2, 768, 128), BF16),
            pltpu.VMEM((256, 128), BF16),
            pltpu.VMEM((144, D), BF16),
            pltpu.VMEM((16, 128), F32),
            pltpu.VMEM((16, 128), F32),
            dma((1,)), dma((1,)), dma((4,)), dma((1,)), dma((2,)), dma((2,)),
            dma((16,)), dma((12,)), dma((1,)), dma((1,)), dma((16,)), dma((16,)),
        ],
        compiler_params=pltpu.CompilerParams(
            collective_id=0, has_side_effects=True, vmem_limit_bytes=60 * 1024 * 1024
        ),
        cost_estimate=pl.CostEstimate(flops=4_000_000_000, bytes_accessed=14_000_000, transcendentals=1_700_000),
    )(
        noise, step_ids, mod_table.transpose(1, 0, 2), embed_weight, qkv_weight,
        q_gain.reshape(1, HD), k_gain.reshape(1, HD), out_weight, final_weight.T,
    )
    return both[None, :, 0:C], both[None, :, C:]


def solution(mesh):
    in_specs = (P("seq", None), P(), P(), P(), P(None, "tm"), P(), P(), P("tm", None), P())
    out_specs = (P("tm", "seq", None), P("tm", "seq", None))
    return jax.shard_map(body, mesh=mesh, in_specs=in_specs, out_specs=out_specs, check_vma=False)
```

time: 71.6 us -> 43.9 us (0.61)
  Pallas kernels: 65.9 us -> 42.4 us
  local copies, waits for them, and re-layouts: 4.86 us -> 0.68 us
    pallas_call x1, Pallas kernels: 65.9 us -> 42.4 us  [body(): pl.pallas_call(kernel, out_shape=out, in_specs=[hbm] * 9, out_specs=vmem,...]
    unnamed x14 -> x0, local copies, waits for them, and re-layouts: 4.86 us -> none
where the time goes in v2:
time: 43.9 us; the launch traced here: 43.8 us
  Pallas kernels  42.4 us (97%)
  local copies, waits for them, and re-layouts  0.68 us (2%)
  between operations  0.64 us (1%)
    pallas_call x1, Pallas kernels, body(): pl.pallas_call(kernel, out_shape=out, in_specs=[hbm] * 9, out_specs=vmem,...  42.4 us

profile of v2, /device:TPU:6, one launch (start us, length us, event | category | flops | bytes accessed | tf_op | source)
XLA Modules:
  0.0 43.8 jit_solution(15509924098689390579)
XLA Ops:
  0.6 42.4 %shard_map.104 = f32[32,128]{1,0:T(8,128)S(1)} custom-call(f32[32,64]{1,0:T(8,128)} %noise_ref.1, s32[5]{0:T(128)} %ids_in.1, f32[3,28,3072]{2,1,0:T(8,128)} %bitcast.8, bf16[64,3072]{1,0:T(8,128)(2,1)} %e_ref.1, bf16[3072,1152]{1,0:T(8,128)(2,1)} %w_ref.1, f32[1,128]{1,0:T(1,128)} %bitcast.10, f32[1,128]{1,0:T(1,128)} %bitcast.11, bf16[384,3072]{1,0:T(8,128)(2,1)} %o_ref.1, ...), custom_call_target="tpu_custom_call" | custom-call | flops 4000000000 | bytes 14000000 | tf_op jit(solution)/shard_map/pallas_call | solution.py:433
  43.1 0.7 %slice_bitcast_fusion = (f32[1,32,64]{2,1,0:T(8,128)}, f32[1,32,64]{2,1,0:T(8,128)}) fusion(f32[32,128]{1,0:T(8,128)S(1)} %shard_map.104), kind=kLoop, calls=%fused_computation | loop fusion | bytes 32768 | tf_op jit(solution)/shard_map/broadcast_in_dim | solution.py:482

commit v3 on v2

v3 whole, which is shorter than its diff:
```python
import math

import jax
import jax.numpy as jnp
from jax import lax
from jax.experimental import pallas as pl
from jax.experimental.pallas import tpu as pltpu
from jax.sharding import PartitionSpec as P

MESH = pl.DeviceIdType.MESH
F32 = jnp.float32
BF16 = jnp.bfloat16
C = 64
D = 3072
HD = 128
HEADS = 3
WINDOW = 4
TOTAL = 28
EPS = 1e-6
PARTS = 6
DEPTH = D // PARTS
COLS = 3 * HD * HEADS
FAR_FIRST = sorted(
    [(a, b) for a in range(8) for b in range(4) if a or b],
    key=lambda ab: -(min(ab[0], 8 - ab[0]) + min(ab[1], 4 - ab[1])),
)
CONTRACT_LAST = (((1,), (1,)), ((), ()))


def dot(left, right):
    return jnp.dot(left, right, preferred_element_type=F32)


def dot_t(left, right):
    return lax.dot_general(left, right, CONTRACT_LAST, preferred_element_type=F32)


def split(value, pieces):
    out = []
    for _ in range(pieces):
        piece = value.astype(BF16)
        out.append(piece)
        value = value - piece.astype(F32)
    return out


def left_half(value):
    return jnp.concatenate([value, jnp.zeros_like(value)], axis=1)


def right_half(value):
    return jnp.concatenate([jnp.zeros_like(value), value], axis=1)


def kernel(
    noise_ref, ids_in, mod_ref, e_ref, w_ref, qgain_ref, kgain_ref, o_ref, f_ref,
    out_ref,
    noise_in, ids_ref, mod_in, e_in, w_in, qg_ref, kg_ref, o_in, f_in, local_sem, w_sem,
    own_noise, red_noise, xb1, xb2, keys_ref, values_ref, queries_ref, part1, part2, box, final_box, zero_sum, zero_box,
    lat_rows,
    proj, wa, wb, bias, g12, g3, nw, efw, a_hi, lat_acc, dr_acc, next_inputs, deltas,
    a_s, a_r, n_s, n_r, h_s, h_r, r_r, b_s, b_r, out_s, out2_s, zero_s, o_r,
):
    c = lax.axis_index("tm")
    s = lax.axis_index("seq")
    z = s // 8
    y = (s // 2) % 4
    core = s % 2

    def device(cc, zz, yy):
        return (cc % 4, (zz % 8) * 8 + (yy % 4) * 2 + core)

    sibling = (c, z * 8 + y * 2 + 1 - core)

    noise_copy = pltpu.make_async_copy(noise_ref, noise_in, local_sem.at[0])
    noise_copy.start()

    barrier = pltpu.get_barrier_semaphore()
    early = z < 4
    worker = jnp.logical_and(early, y < 3)
    half = z // 4
    near_z = jnp.where(early, z, (z + 2) % 4)
    partner = 4 + (z + 2) % 4

    def greet(target):
        pl.semaphore_signal(barrier, inc=1, device_id=target, device_id_type=MESH)

    @pl.when(early)
    def _():
        for dz, dy in FAR_FIRST:
            greet(device(c, z + dz, y + dy))
        for dx in range(1, 4):
            for dy in range(4):
                greet(device(c + dx, z, y + dy))
        greet(sibling)

    copies = [
        pltpu.make_async_copy(e_ref, e_in, local_sem.at[1]),
        pltpu.make_async_copy(ids_in, ids_ref, local_sem.at[2]),
        pltpu.make_async_copy(mod_ref, mod_in, local_sem.at[3]),
        pltpu.make_async_copy(f_ref, f_in, local_sem.at[4]),
        pltpu.make_async_copy(o_ref, o_in, local_sem.at[5]),
        pltpu.make_async_copy(qgain_ref, qg_ref, local_sem.at[6]),
        pltpu.make_async_copy(kgain_ref, kg_ref, local_sem.at[7]),
    ]
    w_copies = [
        pltpu.make_async_copy(
            w_ref.at[pl.ds(n * DEPTH, DEPTH)], w_in.at[pl.ds(n * DEPTH, DEPTH)], w_sem.at[0]
        )
        for n in range(PARTS)
    ]

    def fetch():
        for copy in copies[:3] + w_copies + copies[3:]:
            copy.start()

    def small_matrices():
        copies[0].wait()
        embed = e_in[...].astype(F32)
        centred = embed - jnp.mean(embed, axis=1, keepdims=True)
        copies[1].wait()
        copies[2].wait()
        here = pl.ds(ids_ref[y], 1)
        shift = mod_in[0, here]
        scale = mod_in[1, here]
        gate = mod_in[2, here]
        scaled = split(centred * (1.0 + scale), 2)
        a_hi[0:64] = scaled[0]
        a_hi[64:128] = scaled[1]
        shifts = split(shift, 2)
        row = lax.broadcasted_iota(jnp.int32, (16, D), 0)
        a_hi[128:144] = jnp.where(
            row == 0, jnp.broadcast_to(shift, (16, D)),
            jnp.where(row == 1, jnp.broadcast_to(shift - shifts[0].astype(F32), (16, D)), 0.0),
        ).astype(BF16)

        pieces = split(centred, 3)
        stacked = jnp.concatenate(pieces, axis=0)
        gram = dot_t(stacked, stacked)
        gram = gram[0:64] + gram[64:128] + gram[128:192]
        gram = (gram[:, 0:64] + gram[:, 64:128] + gram[:, 128:192]) * (1.0 / D)
        g1, g2, gl = split(gram, 3)
        g12[0:64] = left_half(g1)
        g12[64:128] = right_half(g1)
        g12[128:192] = left_half(g2)
        g12[192:256] = right_half(g2)
        g3[0:64] = left_half(gl)
        g3[64:128] = right_half(gl)

        pltpu.make_async_copy(w_ref, w_in, w_sem.at[0]).wait()
        proj[...] = dot(a_hi[...], w_in[...])
        small = proj[0:64] + proj[64:128]
        bias[...] = proj[128:136]
        small_hi, small_lo = split(small, 2)
        none = jnp.zeros((64, COLS), BF16)
        for n, value in enumerate((small_hi, none, small_lo, none)):
            wa[n * 64:(n + 1) * 64] = value
        for n, value in enumerate((none, small_hi, none, small_lo)):
            wb[n * 64:(n + 1) * 64] = value

        values_ref[:, :, HD:] = jnp.ones((HEADS, 2048, HD), BF16)
        for copy in copies[3:]:
            copy.wait()
        final = f_in[...]
        final_hl = jnp.concatenate(split(final, 2), axis=0)
        gated_hl = jnp.concatenate(split(final * gate, 2), axis=0)
        head_out = dot_t(o_in[...], gated_hl)
        embed_out = dot_t(e_in[...], final_hl)
        head_out = head_out[:, 0:64] + head_out[:, 64:128]
        own = (c == 0).astype(F32)
        embed_out = (embed_out[:, 0:64] + embed_out[:, 64:128]) * own
        for n, value in enumerate(split(head_out, 2)):
            nw[n, 0:384] = left_half(value)
            nw[n, 384:768] = right_half(value)
        for n, value in enumerate(split(embed_out, 2)):
            efw[n * 128:n * 128 + 64] = left_half(value)
            efw[n * 128 + 64:n * 128 + 128] = right_half(value)

    @pl.when(early)
    def _():
        fetch()

    noise_copy.wait()
    packed = jnp.concatenate([noise_in[0:16], noise_in[16:32]], axis=1)
    own_noise[...] = packed
    slot = half * 16 + near_z * 4 + y
    xb1[core, slot] = packed.astype(BF16)

    @pl.when(early)
    def _():
        pl.semaphore_wait(barrier, 28)

    @pl.when(jnp.logical_not(early))
    def _():
        pl.semaphore_wait(barrier, 16)


    def a_copy(zz, yy):
        return pltpu.make_async_remote_copy(
            src_ref=xb1.at[core, slot], dst_ref=xb1.at[core, slot], send_sem=a_s.at[0], recv_sem=a_r.at[half],
            device_id=device(c, zz, yy), device_id_type=MESH,
        )

    def blocks(buffer, count, send, recv):
        part = buffer.at[core, pl.ds(0, count)]
        return pltpu.make_async_remote_copy(
            src_ref=part, dst_ref=part, send_sem=send, recv_sem=recv, device_id=sibling, device_id_type=MESH,
        )

    @pl.when(early)
    def _():
        for zz in range(4):
            for yy in range(3):
                @pl.when(jnp.logical_not(jnp.logical_and(z == zz, y == yy)))
                def _():
                    a_copy(zz, yy).start()

    @pl.when(jnp.logical_not(early))
    def _():
        for dz in (4, 3, 5, 2, 6, 1, 7):
            @pl.when((z + dz) % 8 < 4)
            def _():
                for yy in range(3):
                    a_copy(z + dz, yy).start()

    def n_copy(t):
        return pltpu.make_async_remote_copy(
            src_ref=own_noise, dst_ref=red_noise.at[half], send_sem=n_s.at[t], recv_sem=n_r.at[half],
            device_id=device(c, near_z, t), device_id_type=MESH,
        )

    @pl.when(y == c)
    def _():
        @pl.when(jnp.logical_and(early, y > 0))
        def _():
            red_noise[0] = own_noise[...]

        for t in range(1, WINDOW):
            @pl.when(jnp.logical_or(y != t, z >= 4))
            def _():
                n_copy(t).start()

    @pl.when(early)
    def _():
        small_matrices()

    @pl.when(jnp.logical_not(early))
    def _():
        copies[1].start()
        copies[1].wait()

    def sigma(n):
        left = 1.0 - jnp.full((16, 128), ids_ref[n]).astype(F32) / TOTAL
        return 3.0 * left / (1.0 + 2.0 * left)

    for t in range(WINDOW):
        deltas[t] = sigma(t + 1) - sigma(t)

    def doubled(x):
        return jnp.concatenate([x, x], axis=1)

    def inverse_deviation(x, xx):
        term = (dot(xx, g12[...]) + dot(x, g3[...])) * x.astype(F32)
        lane = lax.broadcasted_iota(jnp.int32, term.shape, 1)
        first = jnp.sum(jnp.where(lane < 64, term, 0.0), axis=1, keepdims=True)
        second = jnp.sum(jnp.where(lane < 64, 0.0, term), axis=1, keepdims=True)
        return lax.rsqrt(first + EPS), lax.rsqrt(second + EPS)

    def bias_of(start):
        return bias[0:1, start:start + HD] + bias[1:2, start:start + HD]

    def project(x, begin):
        x = x.reshape(x.shape[0] * 16, 128)
        xx = doubled(x)
        va, vb = inverse_deviation(x, xx)
        rows = slice(begin, begin + 2 * x.shape[0])
        for h in range(HEADS):
            start = h * 3 * HD + HD
            kva = dot(xx, wa[:, start:start + 2 * HD]) * va
            kvb = dot(xx, wb[:, start:start + 2 * HD]) * vb
            kv = jnp.concatenate([kva, kvb], axis=0)
            keys = kv[:, 0:HD] + bias_of(start)
            square = jnp.mean(keys * keys, axis=1, keepdims=True)
            keys_ref[h, rows] = (keys * lax.rsqrt(square + EPS)).astype(BF16)
            values_ref[h, rows, 0:HD] = kv[:, HD:].astype(BF16)

    def half_copy(buffer, which, n, index):
        part = buffer.at[which, pl.ds(n * 16, 16)]
        return pltpu.make_async_remote_copy(
            src_ref=part, dst_ref=part, send_sem=h_s.at[index], recv_sem=h_r.at[index],
            device_id=sibling, device_id_type=MESH,
        )

    def make_queries(blocks_in, begin):
        gains = qg_ref[...] * kg_ref[...] * (HD ** -0.5 * math.log2(math.e))
        xq = jnp.concatenate(blocks_in, axis=0)
        xxq = doubled(xq)
        ra, rb = inverse_deviation(xq, xxq)
        for h in range(HEADS):
            start = h * 3 * HD
            qa = dot(xxq, wa[:, start:start + HD]) * ra
            qb = dot(xxq, wb[:, start:start + HD]) * rb
            q = jnp.concatenate([qa, qb], axis=0) + bias_of(start)
            q = q * lax.rsqrt(jnp.mean(q * q, axis=1, keepdims=True) + EPS) * gains
            queries_ref[h, begin:begin + 128] = q.astype(BF16)
        return xxq

    def attend(rows, inputs):
        heads = []
        for h in range(HEADS):
            weights = jnp.exp2(dot_t(queries_ref[h, 0:rows], keys_ref[h])).astype(BF16)
            summed = dot(weights, values_ref[h])
            heads.append((summed[:, 0:HD] / summed[:, HD:] + bias_of((3 * h + 2) * HD)).astype(BF16))
        attention = jnp.concatenate(heads, axis=1)
        out = []
        for n, xxq in enumerate(inputs):
            pair = jnp.concatenate(
                [attention[n * 128:n * 128 + 64], attention[n * 128 + 64:n * 128 + 128]], axis=1
            )
            out.append(
                (dot(pair, nw[0]) + dot(pair, nw[1]) + dot(xxq, efw[...])).reshape(4, 16, 128)
            )
        return out

    def first_sweep():
        blocks(xb1, 15, a_s.at[0], a_r.at[0]).wait_recv()
        half_copy(xb1, core, 0, 0).start()
        xxq = make_queries([xb1[core, z * 4 + i] for i in range(4)], 0)
        project(xb1[core, 0:16], 0)
        half_copy(xb1, 1 - core, 0, 0).wait_recv()
        project(xb1[1 - core, 0:16], 512)
        blocks(xb1, 16, a_s.at[0], a_r.at[1]).wait_recv()
        half_copy(xb1, core, 1, 1).start()
        xxq2 = make_queries([xb1[core, 16 + z * 4 + i] for i in range(4)], 128)
        project(xb1[core, 16:32], 1024)
        half_copy(xb1, 1 - core, 1, 1).wait_recv()
        project(xb1[1 - core, 16:32], 1536)
        first, second = attend(256, (xxq, xxq2))
        part1[0] = first.astype(BF16)
        part1[1] = second.astype(BF16)

    def second_sweep():
        one = z // 2
        two = 1 - one
        blocks(xb2, 14, b_s.at[0], b_r.at[one]).wait_recv()
        half_copy(xb2, core, one, 2).start()
        xxq = make_queries([xb2[core, z * 8 + i * 2] for i in range(4)], 0)
        xxq2 = make_queries([xb2[core, z * 8 + i * 2 + 1] for i in range(4)], 128)
        project(xb2[core, pl.ds(one * 16, 16)], 0)
        blocks(xb2, 16, b_s.at[0], b_r.at[two]).wait_recv()
        half_copy(xb2, core, two, 3).start()
        project(xb2[core, pl.ds(two * 16, 16)], 512)
        half_copy(xb2, 1 - core, one, 2).wait_recv()
        half_copy(xb2, 1 - core, two, 3).wait_recv()
        project(xb2[1 - core], 1024)
        first, second = attend(256, (xxq, xxq2))
        part2[0] = first.astype(BF16)
        part2[1] = second.astype(BF16)

    def r_copy(t, i):
        return pltpu.make_async_remote_copy(
            src_ref=part1.at[:, i], dst_ref=box.at[y * 4 + c], send_sem=out_s.at[0], recv_sem=r_r.at[y],
            device_id=device(i, z, t), device_id_type=MESH,
        )

    def o_copy(t, h, i):
        return pltpu.make_async_remote_copy(
            src_ref=part2.at[h, i], dst_ref=final_box.at[y * 4 + c], send_sem=out2_s.at[0], recv_sem=o_r.at[y],
            device_id=device(t, partner if h else z, i), device_id_type=MESH,
        )

    def zero_copy(t, h):
        return pltpu.make_async_remote_copy(
            src_ref=zero_sum.at[h], dst_ref=zero_box, send_sem=zero_s.at[0], recv_sem=o_r.at[0],
            device_id=device(t, partner if h else z, c), device_id_type=MESH,
        )

    def boxes(count, recv):
        part = box.at[pl.ds(0, count)]
        return pltpu.make_async_remote_copy(
            src_ref=part, dst_ref=part, send_sem=out_s.at[0], recv_sem=recv, device_id=sibling, device_id_type=MESH,
        )

    def final_boxes(count, recv):
        part = final_box.at[pl.ds(0, count)]
        return pltpu.make_async_remote_copy(
            src_ref=part, dst_ref=part, send_sem=out2_s.at[0], recv_sem=recv, device_id=sibling, device_id_type=MESH,
        )

    def send_out():
        for t in range(1, WINDOW):
            @pl.when(t >= y)
            def _():
                for i in range(4):
                    mine = jnp.logical_and(t == c, i == y)
                    o_copy(t, 1, i).start()

                    @pl.when(mine)
                    def _():
                        final_box[y * 4 + c] = part2[0, i]

                    @pl.when(jnp.logical_not(mine))
                    def _():
                        o_copy(t, 0, i).start()

    @pl.when(worker)
    def _():
        first_sweep()
        for t in range(1, WINDOW):
            @pl.when(t > y)
            def _():
                for i in range(4):
                    r_copy(t, i).start()

    @pl.when(jnp.logical_and(early, y > 0))
    def _():
        @pl.when(y != c)
        def _():
            n_copy(0).wait_recv()

        late_noise = pltpu.make_async_remote_copy(
            src_ref=own_noise, dst_ref=red_noise.at[1], send_sem=n_s.at[0], recv_sem=n_r.at[1],
            device_id=sibling, device_id_type=MESH,
        )
        late_noise.wait_recv()
        next_inputs[...] = red_noise[...]
        for t in range(3):
            @pl.when(t < y)
            def _():
                boxes(4, r_r.at[t]).wait_recv()
                total = sum(box[t * 4 + cc].astype(F32) for cc in range(4))
                next_inputs[...] += deltas[t][None] * total
                if t == 0:
                    zero_sum[...] = total
        place = near_z * 8 + c * 2
        xb2[core, pl.ds(place, 2)] = next_inputs[...].astype(BF16)
        part = xb2.at[core, pl.ds(place, 2)]
        for dz in (3, -3, 2, -2, 1, -1, 0):
            @pl.when(jnp.logical_and(z + dz >= 0, z + dz < 4))
            def _():
                for dx in (2, 1, 3, 0):
                    if dx or dz:
                        pltpu.make_async_remote_copy(
                            src_ref=part, dst_ref=part, send_sem=b_s.at[0], recv_sem=b_r.at[z // 2],
                            device_id=device(c + dx, z + dz, y), device_id_type=MESH,
                        ).start()

        @pl.when(y == 1)
        def _():
            for t in range(WINDOW):
                for n in range(2):
                    if t == 1 and n == 0:
                        @pl.when(c != 1)
                        def _():
                            zero_copy(t, n).start()

                        @pl.when(c == 1)
                        def _():
                            zero_box[...] = zero_sum[0]
                    else:
                        zero_copy(t, n).start()

    @pl.when(jnp.logical_and(early, y > 0))
    def _():
        second_sweep()
        send_out()

    @pl.when(worker)
    def _():
        blocks(xb1, 11, a_s.at[0], a_r.at[0]).wait_send()
        half_copy(xb1, core, 0, 0).wait_send()
        half_copy(xb1, core, 1, 1).wait_send()
        for t in range(3):
            @pl.when(y == t)
            def _():
                boxes(4 * (3 - t), r_r.at[0]).wait_send()

    @pl.when(jnp.logical_not(worker))
    def _():
        blocks(xb1, 12, a_s.at[0], a_r.at[0]).wait_send()

    @pl.when(y == c)
    def _():
        for t in range(1, WINDOW):
            @pl.when(jnp.logical_or(y != t, z >= 4))
            def _():
                n_copy(t).wait_send()

    @pl.when(jnp.logical_and(early, y > 0))
    def _():
        part = xb2.at[core, pl.ds(0, 30)]
        pltpu.make_async_remote_copy(
            src_ref=part, dst_ref=part, send_sem=b_s.at[0], recv_sem=b_r.at[0],
            device_id=sibling, device_id_type=MESH,
        ).wait_send()
        half_copy(xb2, core, 0, 2).wait_send()
        half_copy(xb2, core, 1, 3).wait_send()
        for t in range(1, WINDOW):
            for kept in range(2):
                @pl.when(jnp.logical_and(y == t, (c >= t) == jnp.bool_(kept)))
                def _():
                    final_boxes(8 * (4 - t) - kept, o_r.at[0]).wait_send()

        def zero_sent(count):
            part = lat_rows.at[pl.ds(0, count)]
            pltpu.make_async_remote_copy(
                src_ref=part, dst_ref=part, send_sem=zero_s.at[0], recv_sem=o_r.at[0],
                device_id=sibling, device_id_type=MESH,
            ).wait_send()

        @pl.when(jnp.logical_and(y == 1, c == 1))
        def _():
            zero_sent(7)

        @pl.when(jnp.logical_and(y == 1, c != 1))
        def _():
            zero_sent(8)

    lat_acc[...] = own_noise[...]
    for t in range(WINDOW):
        @pl.when(t <= c)
        def _():
            if t == 0:
                @pl.when(jnp.logical_not(jnp.logical_and(early, jnp.logical_and(y == 1, c == 1))))
                def _():
                    pltpu.make_async_remote_copy(
                        src_ref=zero_box, dst_ref=zero_box, send_sem=zero_s.at[0], recv_sem=o_r.at[0],
                        device_id=sibling, device_id_type=MESH,
                    ).wait_recv()

                total = zero_box[...]
            else:
                @pl.when(jnp.logical_and(early, t == y))
                def _():
                    final_boxes(3, o_r.at[t]).wait_recv()

                @pl.when(jnp.logical_not(jnp.logical_and(early, t == y)))
                def _():
                    final_boxes(4, o_r.at[t]).wait_recv()

                first = t * 4
                total = sum(final_box[first + cc].astype(F32) for cc in range(4))
            lat_acc[...] += deltas[t] * total
            dr_acc[...] = total
    out_ref[0:16, 0:C] = lat_acc[:, 0:C]
    out_ref[16:32, 0:C] = lat_acc[:, C:]
    out_ref[0:16, C:] = dr_acc[:, 0:C]
    out_ref[16:32, C:] = dr_acc[:, C:]


def body(
    noise, step_ids, mod_table, embed_weight, qkv_weight, q_gain, k_gain, out_weight, final_weight
):
    hbm = pl.BlockSpec(memory_space=pltpu.HBM)
    vmem = pl.BlockSpec(memory_space=pltpu.VMEM)
    out = pltpu.VMEM((32, 2 * C), F32)
    dma = pltpu.SemaphoreType.DMA
    both = pl.pallas_call(
        kernel,
        out_shape=out,
        in_specs=[hbm] * 9,
        out_specs=vmem,
        scratch_shapes=[
            pltpu.VMEM((32, C), F32),
            pltpu.SMEM((WINDOW + 1,), jnp.int32),
            pltpu.VMEM((3, TOTAL, D), F32),
            pltpu.VMEM((C, D), BF16),
            pltpu.VMEM((D, COLS), BF16),
            pltpu.VMEM((1, HD), F32),
            pltpu.VMEM((1, HD), F32),
            pltpu.VMEM((HEADS * HD, D), BF16),
            pltpu.VMEM((C, D), F32),
            dma((8,)),
            dma((1,)),
            pltpu.VMEM((16, 128), F32),
            pltpu.VMEM((2, 16, 128), F32),
            pltpu.VMEM((2, 32, 16, 128), BF16),
            pltpu.VMEM((2, 32, 16, 128), BF16),
            pltpu.VMEM((HEADS, 2048, HD), BF16),
            pltpu.VMEM((HEADS, 2048, 2 * HD), BF16),
            pltpu.VMEM((HEADS, 256, HD), BF16),
            pltpu.VMEM((2, 4, 16, 128), BF16),
            pltpu.VMEM((2, 4, 16, 128), BF16),
            pltpu.VMEM((12, 2, 16, 128), BF16),
            pltpu.VMEM((24, 16, 128), BF16),
            pltpu.VMEM((2, 16, 128), F32),
            pltpu.VMEM((16, 128), F32),
            pltpu.VMEM((8, 16, 128), F32),
            pltpu.VMEM((144, COLS), F32),
            pltpu.VMEM((256, COLS), BF16),
            pltpu.VMEM((256, COLS), BF16),
            pltpu.VMEM((8, COLS), F32),
            pltpu.VMEM((256, 128), BF16),
            pltpu.VMEM((128, 128), BF16),
            pltpu.VMEM((2, 768, 128), BF16),
            pltpu.VMEM((256, 128), BF16),
            pltpu.VMEM((144, D), BF16),
            pltpu.VMEM((16, 128), F32),
            pltpu.VMEM((16, 128), F32),
            pltpu.VMEM((2, 16, 128), F32),
            pltpu.VMEM((WINDOW, 16, 128), F32),
            dma((1,)), dma((2,)), dma((4,)), dma((2,)), dma((4,)), dma((4,)),
            dma((3,)), dma((1,)), dma((2,)), dma((1,)), dma((1,)), dma((1,)), dma((4,)),
        ],
        compiler_params=pltpu.CompilerParams(
            collective_id=0, has_side_effects=True, vmem_limit_bytes=60 * 1024 * 1024
        ),
        cost_estimate=pl.CostEstimate(flops=4_000_000_000, bytes_accessed=14_000_000, transcendentals=1_700_000),
    )(
        noise, step_ids, mod_table.transpose(1, 0, 2), embed_weight, qkv_weight,
        q_gain.reshape(1, HD), k_gain.reshape(1, HD), out_weight, final_weight.T,
    )
    return both[None, :, 0:C], both[None, :, C:]


def solution(mesh):
    in_specs = (P("seq", None), P(), P(), P(), P(None, "tm"), P(), P(), P("tm", None), P())
    out_specs = (P("tm", "seq", None), P("tm", "seq", None))
    return jax.shard_map(body, mesh=mesh, in_specs=in_specs, out_specs=out_specs, check_vma=False)
```

time: 43.9 us -> 38 us (0.87)
  Pallas kernels: 42.4 us -> 36.3 us
    pallas_call x1, Pallas kernels: 42.4 us -> 36.3 us  [body(): pl.pallas_call(kernel, out_shape=out, in_specs=[hbm] * 9, out_specs=vmem,...]
where the time goes in v3:
time: 38 us; the launch traced here: 37.7 us
  Pallas kernels  36.3 us (96%)
  local copies, waits for them, and re-layouts  0.68 us (2%)
  between operations  0.64 us (2%)
    pallas_call x1, Pallas kernels, body(): pl.pallas_call(kernel, out_shape=out, in_specs=[hbm] * 9, out_specs=vmem,...  36.3 us

profile of v3, /device:TPU:6, one launch (start us, length us, event | category | flops | bytes accessed | tf_op | source)
XLA Modules:
  0.0 37.7 jit_solution(1474099559501388496)
XLA Ops:
  0.6 36.3 %shard_map.104 = f32[32,128]{1,0:T(8,128)S(1)} custom-call(f32[32,64]{1,0:T(8,128)} %noise_ref.1, s32[5]{0:T(128)} %ids_in.1, f32[3,28,3072]{2,1,0:T(8,128)} %bitcast.8, bf16[64,3072]{1,0:T(8,128)(2,1)} %e_ref.1, bf16[3072,1152]{1,0:T(8,128)(2,1)} %w_ref.1, f32[1,128]{1,0:T(1,128)} %bitcast.10, f32[1,128]{1,0:T(1,128)} %bitcast.11, bf16[384,3072]{1,0:T(8,128)(2,1)} %o_ref.1, ...), custom_call_target="tpu_custom_call" | custom-call | flops 4000000000 | bytes 14000000 | tf_op jit(solution)/shard_map/pallas_call | solution.py:558
  37.0 0.7 %slice_bitcast_fusion = (f32[1,32,64]{2,1,0:T(8,128)}, f32[1,32,64]{2,1,0:T(8,128)}) fusion(f32[32,128]{1,0:T(8,128)S(1)} %shard_map.104), kind=kLoop, calls=%fused_computation | loop fusion | bytes 32768 | tf_op jit(solution)/shard_map/broadcast_in_dim | solution.py:613

commit v4 on v3

--- a/solution.py
+++ b/solution.py
@@ -56,7 +56,7 @@
     noise_ref, ids_in, mod_ref, e_ref, w_ref, qgain_ref, kgain_ref, o_ref, f_ref,
     out_ref,
     noise_in, ids_ref, mod_in, e_in, w_in, qg_ref, kg_ref, o_in, f_in, local_sem, w_sem,
-    own_noise, red_noise, xb1, xb2, keys_ref, values_ref, queries_ref, part1, part2, box, final_box, zero_sum, zero_box,
+    own_noise, red_noise, xb1, xb2, keys_ref, values_ref, queries_ref, early_sum, part1, part2, box, final_box, zero_sum, zero_box,
     lat_rows,
     proj, wa, wb, bias, g12, g3, nw, efw, a_hi, lat_acc, dr_acc, next_inputs, deltas,
     a_s, a_r, n_s, n_r, h_s, h_r, r_r, b_s, b_r, out_s, out2_s, zero_s, o_r,
@@ -111,15 +111,14 @@
     ]
 
     def fetch():
-        for copy in copies[:3] + w_copies + copies[3:]:
+        for copy in copies + w_copies:
             copy.start()
 
     def small_matrices():
-        copies[0].wait()
+        for copy in copies[:3]:
+            copy.wait()
         embed = e_in[...].astype(F32)
         centred = embed - jnp.mean(embed, axis=1, keepdims=True)
-        copies[1].wait()
-        copies[2].wait()
         here = pl.ds(ids_ref[y], 1)
         shift = mod_in[0, here]
         scale = mod_in[1, here]
@@ -147,18 +146,6 @@
         g3[0:64] = left_half(gl)
         g3[64:128] = right_half(gl)
 
-        pltpu.make_async_copy(w_ref, w_in, w_sem.at[0]).wait()
-        proj[...] = dot(a_hi[...], w_in[...])
-        small = proj[0:64] + proj[64:128]
-        bias[...] = proj[128:136]
-        small_hi, small_lo = split(small, 2)
-        none = jnp.zeros((64, COLS), BF16)
-        for n, value in enumerate((small_hi, none, small_lo, none)):
-            wa[n * 64:(n + 1) * 64] = value
-        for n, value in enumerate((none, small_hi, none, small_lo)):
-            wb[n * 64:(n + 1) * 64] = value
-
-        values_ref[:, :, HD:] = jnp.ones((HEADS, 2048, HD), BF16)
         for copy in copies[3:]:
             copy.wait()
         final = f_in[...]
@@ -175,10 +162,21 @@
         for n, value in enumerate(split(embed_out, 2)):
             efw[n * 128:n * 128 + 64] = left_half(value)
             efw[n * 128 + 64:n * 128 + 128] = right_half(value)
+        pltpu.make_async_copy(w_ref, w_in, w_sem.at[0]).wait()
+        proj[...] = dot(a_hi[...], w_in[...])
+        small = proj[0:64] + proj[64:128]
+        bias[...] = proj[128:136]
+        small_hi, small_lo = split(small, 2)
+        none = jnp.zeros((64, COLS), BF16)
+        for n, value in enumerate((small_hi, none, small_lo, none)):
+            wa[n * 64:(n + 1) * 64] = value
+        for n, value in enumerate((none, small_hi, none, small_lo)):
+            wb[n * 64:(n + 1) * 64] = value
 
     @pl.when(early)
     def _():
         fetch()
+        values_ref[:, :, HD:] = jnp.ones((HEADS, 2048, HD), BF16)
 
     noise_copy.wait()
     packed = jnp.concatenate([noise_in[0:16], noise_in[16:32]], axis=1)
@@ -305,22 +303,20 @@
             queries_ref[h, begin:begin + 128] = q.astype(BF16)
         return xxq
 
-    def attend(rows, inputs):
+    def weighted(h, rows, keys):
+        weights = jnp.exp2(dot_t(queries_ref[h, rows], keys_ref[h, keys])).astype(BF16)
+        return dot(weights, values_ref[h, keys])
+
+    def finish(sums, xxq):
         heads = []
-        for h in range(HEADS):
-            weights = jnp.exp2(dot_t(queries_ref[h, 0:rows], keys_ref[h])).astype(BF16)
-            summed = dot(weights, values_ref[h])
+        for h, summed in enumerate(sums):
             heads.append((summed[:, 0:HD] / summed[:, HD:] + bias_of((3 * h + 2) * HD)).astype(BF16))
         attention = jnp.concatenate(heads, axis=1)
-        out = []
-        for n, xxq in enumerate(inputs):
-            pair = jnp.concatenate(
-                [attention[n * 128:n * 128 + 64], attention[n * 128 + 64:n * 128 + 128]], axis=1
-            )
-            out.append(
-                (dot(pair, nw[0]) + dot(pair, nw[1]) + dot(xxq, efw[...])).reshape(4, 16, 128)
-            )
-        return out
+        pair = jnp.concatenate([attention[0:64], attention[64:128]], axis=1)
+        result = dot(pair, nw[0]) + dot(pair, nw[1]) + dot(xxq, efw[...])
+        return result.reshape(4, 16, 128).astype(BF16)
+
+    low, high, every = slice(0, 128), slice(128, 256), slice(0, 2048)
 
     def first_sweep():
         blocks(xb1, 15, a_s.at[0], a_r.at[0]).wait_recv()
@@ -329,15 +325,18 @@
         project(xb1[core, 0:16], 0)
         half_copy(xb1, 1 - core, 0, 0).wait_recv()
         project(xb1[1 - core, 0:16], 512)
+        for h in range(HEADS):
+            early_sum[h] = weighted(h, low, slice(0, 1024))
         blocks(xb1, 16, a_s.at[0], a_r.at[1]).wait_recv()
         half_copy(xb1, core, 1, 1).start()
         xxq2 = make_queries([xb1[core, 16 + z * 4 + i] for i in range(4)], 128)
         project(xb1[core, 16:32], 1024)
         half_copy(xb1, 1 - core, 1, 1).wait_recv()
         project(xb1[1 - core, 16:32], 1536)
-        first, second = attend(256, (xxq, xxq2))
-        part1[0] = first.astype(BF16)
-        part1[1] = second.astype(BF16)
+        first = [early_sum[h] + weighted(h, low, slice(1024, 2048)) for h in range(HEADS)]
+        second = [weighted(h, high, every) for h in range(HEADS)]
+        part1[0] = finish(first, xxq)
+        part1[1] = finish(second, xxq2)
 
     def second_sweep():
         one = z // 2
@@ -345,17 +344,18 @@
         blocks(xb2, 14, b_s.at[0], b_r.at[one]).wait_recv()
         half_copy(xb2, core, one, 2).start()
         xxq = make_queries([xb2[core, z * 8 + i * 2] for i in range(4)], 0)
-        xxq2 = make_queries([xb2[core, z * 8 + i * 2 + 1] for i in range(4)], 128)
         project(xb2[core, pl.ds(one * 16, 16)], 0)
         blocks(xb2, 16, b_s.at[0], b_r.at[two]).wait_recv()
         half_copy(xb2, core, two, 3).start()
-        project(xb2[core, pl.ds(two * 16, 16)], 512)
         half_copy(xb2, 1 - core, one, 2).wait_recv()
+        project(jnp.concatenate([xb2[1 - core, pl.ds(one * 16, 16)], xb2[core, pl.ds(two * 16, 16)]], axis=0), 512)
         half_copy(xb2, 1 - core, two, 3).wait_recv()
-        project(xb2[1 - core], 1024)
-        first, second = attend(256, (xxq, xxq2))
-        part2[0] = first.astype(BF16)
-        part2[1] = second.astype(BF16)
+        project(xb2[1 - core, pl.ds(two * 16, 16)], 1536)
+        part2[0] = finish([weighted(h, low, every) for h in range(HEADS)], xxq)
+        send_out(0)
+        xxq2 = make_queries([xb2[core, z * 8 + i * 2 + 1] for i in range(4)], 128)
+        part2[1] = finish([weighted(h, high, every) for h in range(HEADS)], xxq2)
+        send_out(1)
 
     def r_copy(t, i):
         return pltpu.make_async_remote_copy(
@@ -387,13 +387,15 @@
             src_ref=part, dst_ref=part, send_sem=out2_s.at[0], recv_sem=recv, device_id=sibling, device_id_type=MESH,
         )
 
-    def send_out():
+    def send_out(h):
         for t in range(1, WINDOW):
             @pl.when(t >= y)
             def _():
                 for i in range(4):
+                    if h:
+                        o_copy(t, h, i).start()
+                        continue
                     mine = jnp.logical_and(t == c, i == y)
-                    o_copy(t, 1, i).start()
 
                     @pl.when(mine)
                     def _():
@@ -401,7 +403,7 @@
 
                     @pl.when(jnp.logical_not(mine))
                     def _():
-                        o_copy(t, 0, i).start()
+                        o_copy(t, h, i).start()
 
     @pl.when(worker)
     def _():
@@ -463,7 +465,6 @@
     @pl.when(jnp.logical_and(early, y > 0))
     def _():
         second_sweep()
-        send_out()
 
     @pl.when(worker)
     def _():
@@ -579,6 +580,7 @@
             pltpu.VMEM((HEADS, 2048, HD), BF16),
             pltpu.VMEM((HEADS, 2048, 2 * HD), BF16),
             pltpu.VMEM((HEADS, 256, HD), BF16),
+            pltpu.VMEM((HEADS, 128, 2 * HD), F32),
             pltpu.VMEM((2, 4, 16, 128), BF16),
             pltpu.VMEM((2, 4, 16, 128), BF16),
             pltpu.VMEM((12, 2, 16, 128), BF16),

time: 38 us -> 36.3 us (0.955)
  Pallas kernels: 36.3 us -> 34.9 us
    pallas_call x1, Pallas kernels: 36.3 us -> 34.9 us  [body(): pl.pallas_call(kernel, out_shape=out, in_specs=[hbm] * 9, out_specs=vmem,...]
where the time goes in v4:
time: 36.3 us; the launch traced here: 36.2 us
  Pallas kernels  34.9 us (96%)
  local copies, waits for them, and re-layouts  0.68 us (2%)
  between operations  0.64 us (2%)
    pallas_call x1, Pallas kernels, body(): pl.pallas_call(kernel, out_shape=out, in_specs=[hbm] * 9, out_specs=vmem,...  34.9 us

profile of v4, /device:TPU:6, one launch (start us, length us, event | category | flops | bytes accessed | tf_op | source)
XLA Modules:
  0.0 36.2 jit_solution(16456440297241277322)
XLA Ops:
  0.6 34.9 %shard_map.104 = f32[32,128]{1,0:T(8,128)S(1)} custom-call(f32[32,64]{1,0:T(8,128)} %noise_ref.1, s32[5]{0:T(128)} %ids_in.1, f32[3,28,3072]{2,1,0:T(8,128)} %bitcast.8, bf16[64,3072]{1,0:T(8,128)(2,1)} %e_ref.1, bf16[3072,1152]{1,0:T(8,128)(2,1)} %w_ref.1, f32[1,128]{1,0:T(1,128)} %bitcast.10, f32[1,128]{1,0:T(1,128)} %bitcast.11, bf16[384,3072]{1,0:T(8,128)(2,1)} %o_ref.1, ...), custom_call_target="tpu_custom_call" | custom-call | flops 4000000000 | bytes 14000000 | tf_op jit(solution)/shard_map/pallas_call | solution.py:559
  35.5 0.7 %slice_bitcast_fusion = (f32[1,32,64]{2,1,0:T(8,128)}, f32[1,32,64]{2,1,0:T(8,128)}) fusion(f32[32,128]{1,0:T(8,128)S(1)} %shard_map.104), kind=kLoop, calls=%fused_computation | loop fusion | bytes 32768 | tf_op jit(solution)/shard_map/broadcast_in_dim | solution.py:615

commit v5 on v4

--- a/solution.py
+++ b/solution.py
@@ -87,8 +87,17 @@
 
     @pl.when(early)
     def _():
-        for dz, dy in FAR_FIRST:
-            greet(device(c, z + dz, y + dy))
+        for n in (4, 5, 6, 7):
+            for dy in (2, 1, 3, 0):
+                greet(device(c, n, y + dy))
+        for n in range(4):
+            for dy in (2, 1, 3, 0):
+                if dy:
+                    greet(device(c, n, y + dy))
+                else:
+                    @pl.when(z != n)
+                    def _():
+                        greet(device(c, n, y))
         for dx in range(1, 4):
             for dy in range(4):
                 greet(device(c + dx, z, y + dy))
@@ -223,7 +232,7 @@
 
     def n_copy(t):
         return pltpu.make_async_remote_copy(
-            src_ref=own_noise, dst_ref=red_noise.at[half], send_sem=n_s.at[t], recv_sem=n_r.at[half],
+            src_ref=own_noise, dst_ref=red_noise.at[half], send_sem=n_s.at[0], recv_sem=n_r.at[half],
             device_id=device(c, near_z, t), device_id_type=MESH,
         )
 
@@ -285,7 +294,7 @@
     def half_copy(buffer, which, n, index):
         part = buffer.at[which, pl.ds(n * 16, 16)]
         return pltpu.make_async_remote_copy(
-            src_ref=part, dst_ref=part, send_sem=h_s.at[index], recv_sem=h_r.at[index],
+            src_ref=part, dst_ref=part, send_sem=h_s.at[0], recv_sem=h_r.at[index],
             device_id=sibling, device_id_type=MESH,
         )
 
@@ -326,15 +335,17 @@
         half_copy(xb1, 1 - core, 0, 0).wait_recv()
         project(xb1[1 - core, 0:16], 512)
         for h in range(HEADS):
-            early_sum[h] = weighted(h, low, slice(0, 1024))
+            early_sum[0, h] = weighted(h, low, slice(0, 1024))
         blocks(xb1, 16, a_s.at[0], a_r.at[1]).wait_recv()
         half_copy(xb1, core, 1, 1).start()
         xxq2 = make_queries([xb1[core, 16 + z * 4 + i] for i in range(4)], 128)
         project(xb1[core, 16:32], 1024)
+        for h in range(HEADS):
+            early_sum[1, h] = weighted(h, high, slice(0, 1024))
         half_copy(xb1, 1 - core, 1, 1).wait_recv()
         project(xb1[1 - core, 16:32], 1536)
-        first = [early_sum[h] + weighted(h, low, slice(1024, 2048)) for h in range(HEADS)]
-        second = [weighted(h, high, every) for h in range(HEADS)]
+        first = [early_sum[0, h] + weighted(h, low, slice(1024, 2048)) for h in range(HEADS)]
+        second = [early_sum[1, h] + weighted(h, high, slice(1024, 2048)) for h in range(HEADS)]
         part1[0] = finish(first, xxq)
         part1[1] = finish(second, xxq2)
 
@@ -388,7 +399,7 @@
         )
 
     def send_out(h):
-        for t in range(1, WINDOW):
+        for t in (3, 2, 1):
             @pl.when(t >= y)
             def _():
                 for i in range(4):
@@ -469,8 +480,6 @@
     @pl.when(worker)
     def _():
         blocks(xb1, 11, a_s.at[0], a_r.at[0]).wait_send()
-        half_copy(xb1, core, 0, 0).wait_send()
-        half_copy(xb1, core, 1, 1).wait_send()
         for t in range(3):
             @pl.when(y == t)
             def _():
@@ -480,12 +489,38 @@
     def _():
         blocks(xb1, 12, a_s.at[0], a_r.at[0]).wait_send()
 
+    def halves(part):
+        pltpu.make_async_remote_copy(
+            src_ref=part, dst_ref=part, send_sem=h_s.at[0], recv_sem=h_r.at[0],
+            device_id=sibling, device_id_type=MESH,
+        ).wait_send()
+
+    both_sweeps = jnp.logical_and(y > 0, y < 3)
+
+    @pl.when(jnp.logical_and(early, both_sweeps))
+    def _():
+        halves(xb1)
+
+    @pl.when(jnp.logical_and(early, jnp.logical_not(both_sweeps)))
+    def _():
+        halves(xb1.at[0])
+
+    def rows(count, send):
+        part = lat_rows.at[pl.ds(0, count)]
+        return pltpu.make_async_remote_copy(
+            src_ref=part, dst_ref=part, send_sem=send, recv_sem=o_r.at[0],
+            device_id=sibling, device_id_type=MESH,
+        )
+
     @pl.when(y == c)
     def _():
-        for t in range(1, WINDOW):
-            @pl.when(jnp.logical_or(y != t, z >= 4))
-            def _():
-                n_copy(t).wait_send()
+        @pl.when(jnp.logical_and(early, y > 0))
+        def _():
+            rows(2, n_s.at[0]).wait_send()
+
+        @pl.when(jnp.logical_not(jnp.logical_and(early, y > 0)))
+        def _():
+            rows(3, n_s.at[0]).wait_send()
 
     @pl.when(jnp.logical_and(early, y > 0))
     def _():
@@ -494,28 +529,19 @@
             src_ref=part, dst_ref=part, send_sem=b_s.at[0], recv_sem=b_r.at[0],
             device_id=sibling, device_id_type=MESH,
         ).wait_send()
-        half_copy(xb2, core, 0, 2).wait_send()
-        half_copy(xb2, core, 1, 3).wait_send()
         for t in range(1, WINDOW):
             for kept in range(2):
                 @pl.when(jnp.logical_and(y == t, (c >= t) == jnp.bool_(kept)))
                 def _():
                     final_boxes(8 * (4 - t) - kept, o_r.at[0]).wait_send()
 
-        def zero_sent(count):
-            part = lat_rows.at[pl.ds(0, count)]
-            pltpu.make_async_remote_copy(
-                src_ref=part, dst_ref=part, send_sem=zero_s.at[0], recv_sem=o_r.at[0],
-                device_id=sibling, device_id_type=MESH,
-            ).wait_send()
-
         @pl.when(jnp.logical_and(y == 1, c == 1))
         def _():
-            zero_sent(7)
+            rows(7, zero_s.at[0]).wait_send()
 
         @pl.when(jnp.logical_and(y == 1, c != 1))
         def _():
-            zero_sent(8)
+            rows(8, zero_s.at[0]).wait_send()
 
     lat_acc[...] = own_noise[...]
     for t in range(WINDOW):
@@ -580,7 +606,7 @@
             pltpu.VMEM((HEADS, 2048, HD), BF16),
             pltpu.VMEM((HEADS, 2048, 2 * HD), BF16),
             pltpu.VMEM((HEADS, 256, HD), BF16),
-            pltpu.VMEM((HEADS, 128, 2 * HD), F32),
+            pltpu.VMEM((2, HEADS, 128, 2 * HD), F32),
             pltpu.VMEM((2, 4, 16, 128), BF16),
             pltpu.VMEM((2, 4, 16, 128), BF16),
             pltpu.VMEM((12, 2, 16, 128), BF16),
@@ -601,7 +627,7 @@
             pltpu.VMEM((16, 128), F32),
             pltpu.VMEM((2, 16, 128), F32),
             pltpu.VMEM((WINDOW, 16, 128), F32),
-            dma((1,)), dma((2,)), dma((4,)), dma((2,)), dma((4,)), dma((4,)),
+            dma((1,)), dma((2,)), dma((1,)), dma((2,)), dma((1,)), dma((4,)),
             dma((3,)), dma((1,)), dma((2,)), dma((1,)), dma((1,)), dma((1,)), dma((4,)),
         ],
         compiler_params=pltpu.CompilerParams(

time: 36.3 us -> 35.9 us (0.989)
  Pallas kernels: 34.9 us -> 34.3 us
    pallas_call x1, Pallas kernels: 34.9 us -> 34.3 us  [body(): pl.pallas_call(kernel, out_shape=out, in_specs=[hbm] * 9, out_specs=vmem,...]
where the time goes in v5:
time: 35.9 us; the launch traced here: 35.6 us
  Pallas kernels  34.3 us (96%)
  local copies, waits for them, and re-layouts  0.68 us (2%)
  between operations  0.64 us (2%)
    pallas_call x1, Pallas kernels, body(): pl.pallas_call(kernel, out_shape=out, in_specs=[hbm] * 9, out_specs=vmem,...  34.3 us

profile of v5, /device:TPU:6, one launch (start us, length us, event | category | flops | bytes accessed | tf_op | source)
XLA Modules:
  0.0 35.6 jit_solution(2888690465738400965)
XLA Ops:
  0.6 34.3 %shard_map.104 = f32[32,128]{1,0:T(8,128)S(1)} custom-call(f32[32,64]{1,0:T(8,128)} %noise_ref.1, s32[5]{0:T(128)} %ids_in.1, f32[3,28,3072]{2,1,0:T(8,128)} %bitcast.8, bf16[64,3072]{1,0:T(8,128)(2,1)} %e_ref.1, bf16[3072,1152]{1,0:T(8,128)(2,1)} %w_ref.1, f32[1,128]{1,0:T(1,128)} %bitcast.10, f32[1,128]{1,0:T(1,128)} %bitcast.11, bf16[384,3072]{1,0:T(8,128)(2,1)} %o_ref.1, ...), custom_call_target="tpu_custom_call" | custom-call | flops 4000000000 | bytes 14000000 | tf_op jit(solution)/shard_map/pallas_call | solution.py:585
  34.9 0.7 %slice_bitcast_fusion = (f32[1,32,64]{2,1,0:T(8,128)}, f32[1,32,64]{2,1,0:T(8,128)}) fusion(f32[32,128]{1,0:T(8,128)S(1)} %shard_map.104), kind=kLoop, calls=%fused_computation | loop fusion | bytes 32768 | tf_op jit(solution)/shard_map/broadcast_in_dim | solution.py:641

commit v6 on v5

--- a/solution.py
+++ b/solution.py
@@ -201,7 +201,6 @@
     def _():
         pl.semaphore_wait(barrier, 16)
 
-
     def a_copy(zz, yy):
         return pltpu.make_async_remote_copy(
             src_ref=xb1.at[core, slot], dst_ref=xb1.at[core, slot], send_sem=a_s.at[0], recv_sem=a_r.at[half],
@@ -271,7 +270,7 @@
         lane = lax.broadcasted_iota(jnp.int32, term.shape, 1)
         first = jnp.sum(jnp.where(lane < 64, term, 0.0), axis=1, keepdims=True)
         second = jnp.sum(jnp.where(lane < 64, 0.0, term), axis=1, keepdims=True)
-        return lax.rsqrt(first + EPS), lax.rsqrt(second + EPS)
+        return lax.rsqrt(jnp.maximum(first, 0.0) + EPS), lax.rsqrt(jnp.maximum(second, 0.0) + EPS)
 
     def bias_of(start):
         return bias[0:1, start:start + HD] + bias[1:2, start:start + HD]

time: 35.9 us -> 35.8 us (level)
  no operation moved by 1% of the time
where the time goes in v6:
time: 35.8 us; the launch traced here: 35.6 us
  Pallas kernels  34.3 us (96%)
  local copies, waits for them, and re-layouts  0.68 us (2%)
  between operations  0.64 us (2%)
    pallas_call x1, Pallas kernels, body(): pl.pallas_call(kernel, out_shape=out, in_specs=[hbm] * 9, out_specs=vmem,...  34.3 us

profile of v6, /device:TPU:6, one launch (start us, length us, event | category | flops | bytes accessed | tf_op | source)
XLA Modules:
  0.0 35.6 jit_solution(869328497056551686)
XLA Ops:
  0.6 34.3 %shard_map.104 = f32[32,128]{1,0:T(8,128)S(1)} custom-call(f32[32,64]{1,0:T(8,128)} %noise_ref.1, s32[5]{0:T(128)} %ids_in.1, f32[3,28,3072]{2,1,0:T(8,128)} %bitcast.8, bf16[64,3072]{1,0:T(8,128)(2,1)} %e_ref.1, bf16[3072,1152]{1,0:T(8,128)(2,1)} %w_ref.1, f32[1,128]{1,0:T(1,128)} %bitcast.10, f32[1,128]{1,0:T(1,128)} %bitcast.11, bf16[384,3072]{1,0:T(8,128)(2,1)} %o_ref.1, ...), custom_call_target="tpu_custom_call" | custom-call | flops 4000000000 | bytes 14000000 | tf_op jit(solution)/shard_map/pallas_call | solution.py:584
  34.9 0.7 %slice_bitcast_fusion = (f32[1,32,64]{2,1,0:T(8,128)}, f32[1,32,64]{2,1,0:T(8,128)}) fusion(f32[32,128]{1,0:T(8,128)S(1)} %shard_map.104), kind=kLoop, calls=%fused_computation | loop fusion | bytes 32768 | tf_op jit(solution)/shard_map/broadcast_in_dim | solution.py:640

commit v7 on v6

--- a/solution.py
+++ b/solution.py
@@ -348,12 +348,12 @@
         part1[0] = finish(first, xxq)
         part1[1] = finish(second, xxq2)
 
-    def second_sweep():
+    def second_sweep(unit):
         one = z // 2
         two = 1 - one
         blocks(xb2, 14, b_s.at[0], b_r.at[one]).wait_recv()
         half_copy(xb2, core, one, 2).start()
-        xxq = make_queries([xb2[core, z * 8 + i * 2] for i in range(4)], 0)
+        xxq = make_queries([xb2[core, z * 8 + i * 2 + unit] for i in range(4)], 0)
         project(xb2[core, pl.ds(one * 16, 16)], 0)
         blocks(xb2, 16, b_s.at[0], b_r.at[two]).wait_recv()
         half_copy(xb2, core, two, 3).start()
@@ -361,11 +361,11 @@
         project(jnp.concatenate([xb2[1 - core, pl.ds(one * 16, 16)], xb2[core, pl.ds(two * 16, 16)]], axis=0), 512)
         half_copy(xb2, 1 - core, two, 3).wait_recv()
         project(xb2[1 - core, pl.ds(two * 16, 16)], 1536)
-        part2[0] = finish([weighted(h, low, every) for h in range(HEADS)], xxq)
-        send_out(0)
-        xxq2 = make_queries([xb2[core, z * 8 + i * 2 + 1] for i in range(4)], 128)
-        part2[1] = finish([weighted(h, high, every) for h in range(HEADS)], xxq2)
-        send_out(1)
+        part2[unit] = finish([weighted(h, low, every) for h in range(HEADS)], xxq)
+        send_out(unit)
+        xxq2 = make_queries([xb2[core, z * 8 + i * 2 + 1 - unit] for i in range(4)], 128)
+        part2[1 - unit] = finish([weighted(h, high, every) for h in range(HEADS)], xxq2)
+        send_out(1 - unit)
 
     def r_copy(t, i):
         return pltpu.make_async_remote_copy(
@@ -474,7 +474,13 @@
 
     @pl.when(jnp.logical_and(early, y > 0))
     def _():
-        second_sweep()
+        @pl.when(z < 3)
+        def _():
+            second_sweep(0)
+
+        @pl.when(z == 3)
+        def _():
+            second_sweep(1)
 
     @pl.when(worker)
     def _():

time: 35.8 us -> 35.8 us (level)
  no operation moved by 1% of the time
where the time goes in v7:
time: 35.8 us; the launch traced here: 35.6 us
  Pallas kernels  34.3 us (96%)
  local copies, waits for them, and re-layouts  0.68 us (2%)
  between operations  0.64 us (2%)
    pallas_call x1, Pallas kernels, body(): pl.pallas_call(kernel, out_shape=out, in_specs=[hbm] * 9, out_specs=vmem,...  34.3 us

profile of v7, /device:TPU:6, one launch (start us, length us, event | category | flops | bytes accessed | tf_op | source)
XLA Modules:
  0.0 35.6 jit_solution(17788456848198042530)
XLA Ops:
  0.6 34.3 %shard_map.104 = f32[32,128]{1,0:T(8,128)S(1)} custom-call(f32[32,64]{1,0:T(8,128)} %noise_ref.1, s32[5]{0:T(128)} %ids_in.1, f32[3,28,3072]{2,1,0:T(8,128)} %bitcast.8, bf16[64,3072]{1,0:T(8,128)(2,1)} %e_ref.1, bf16[3072,1152]{1,0:T(8,128)(2,1)} %w_ref.1, f32[1,128]{1,0:T(1,128)} %bitcast.10, f32[1,128]{1,0:T(1,128)} %bitcast.11, bf16[384,3072]{1,0:T(8,128)(2,1)} %o_ref.1, ...), custom_call_target="tpu_custom_call" | custom-call | flops 4000000000 | bytes 14000000 | tf_op jit(solution)/shard_map/pallas_call | solution.py:590
  34.9 0.7 %slice_bitcast_fusion = (f32[1,32,64]{2,1,0:T(8,128)}, f32[1,32,64]{2,1,0:T(8,128)}) fusion(f32[32,128]{1,0:T(8,128)S(1)} %shard_map.104), kind=kLoop, calls=%fused_computation | loop fusion | bytes 32768 | tf_op jit(solution)/shard_map/broadcast_in_dim | solution.py:646

commit v8 on v7

--- a/solution.py
+++ b/solution.py
@@ -87,7 +87,7 @@
 
     @pl.when(early)
     def _():
-        for n in (4, 5, 6, 7):
+        for n in (7, 6, 5, 4):
             for dy in (2, 1, 3, 0):
                 greet(device(c, n, y + dy))
         for n in range(4):

time: 35.8 us -> 35.8 us (level)
  no operation moved by 1% of the time
where the time goes in v8:
time: 35.8 us; the launch traced here: 35.6 us
  Pallas kernels  34.3 us (96%)
  local copies, waits for them, and re-layouts  0.68 us (2%)
  between operations  0.64 us (2%)
    pallas_call x1, Pallas kernels, body(): pl.pallas_call(kernel, out_shape=out, in_specs=[hbm] * 9, out_specs=vmem,...  34.3 us

profile of v8, /device:TPU:6, one launch (start us, length us, event | category | flops | bytes accessed | tf_op | source)
XLA Modules:
  0.0 35.6 jit_solution(5372981093474913173)
XLA Ops:
  0.6 34.3 %shard_map.104 = f32[32,128]{1,0:T(8,128)S(1)} custom-call(f32[32,64]{1,0:T(8,128)} %noise_ref.1, s32[5]{0:T(128)} %ids_in.1, f32[3,28,3072]{2,1,0:T(8,128)} %bitcast.8, bf16[64,3072]{1,0:T(8,128)(2,1)} %e_ref.1, bf16[3072,1152]{1,0:T(8,128)(2,1)} %w_ref.1, f32[1,128]{1,0:T(1,128)} %bitcast.10, f32[1,128]{1,0:T(1,128)} %bitcast.11, bf16[384,3072]{1,0:T(8,128)(2,1)} %o_ref.1, ...), custom_call_target="tpu_custom_call" | custom-call | flops 4000000000 | bytes 14000000 | tf_op jit(solution)/shard_map/pallas_call | solution.py:590
  34.9 0.7 %slice_bitcast_fusion = (f32[1,32,64]{2,1,0:T(8,128)}, f32[1,32,64]{2,1,0:T(8,128)}) fusion(f32[32,128]{1,0:T(8,128)S(1)} %shard_map.104), kind=kLoop, calls=%fused_computation | loop fusion | bytes 32768 | tf_op jit(solution)/shard_map/broadcast_in_dim | solution.py:646
